TPU v7x, 512 devices: a whole 4x4x16 slice. The times are simulated.
512 devices in a mesh: tm: 64 (over y, z), grp: 8 (over x, core).
Axes of the slice: x: 4, y: 4, z: 16, core: 2. Of those that a mesh axis runs over, the one named last changes fastest.
Arguments:
- records: bfloat16 [2048, 8192], P(('tm', 'grp'))
- band_edges: int32 [4, 2], replicated, may hold values from 2 to 118, as said below
- receiver_block: int32 [64, 9], P('tm'), may hold values from 0 to 63, as said below
- slot_count: int32 [64], P('tm'), may hold values from 5 to 9, as said below
Outputs:
- correlations: float32 [576, 128, 2001], P('tm', 'grp')
Inputs may be any that keep to these rules, and one draw needn't show every extreme that they name: Band b passes from band_edges[b, 0] to band_edges[b, 1] in units of 1/256 cycle a sample; the lower edge is below the upper one by 8 or more. `receiver_block`: each receiver block lies within 4 blocks of its source block o (the row index); both distances 4 and - 4 occur in live slots. Slots k < slot_count[o] are live, the others unused; some source block uses all 9 slots.
All inputs are finite; a program needn't handle non-finite values.
Results may differ from a plain program's by a relative error of at most 0.0033.
Values may be sent and summed in bfloat16 or wider, within the bound.
No kernel may reach another device: no remote copies, remote signals or barrier semaphores. Data moves between devices by JAX's collectives and lax.ppermute only.
A program may use at most 64 MiB of HBM per device.

v0:
```python
import math

import jax
import jax.numpy as jnp
from jax import lax
from jax.experimental import pallas as pl
from jax.experimental.pallas import tpu as pltpu
from jax.sharding import PartitionSpec as P

TAPS = 101
NB = 4
LAG = 1000
R = 4
PMAX = 9
HALF = 50
LAGS = 2001
SAMPLES = 2048
SHIFT = 24
VMEM_LIMIT = 48 * 1024 * 1024


def taps_row(band_edges):
    tap = 178 - jnp.arange(384)
    sample_index = tap.astype(jnp.float32)
    offset = sample_index - HALF
    frequency = band_edges.astype(jnp.float32) / 256.0
    lower = frequency[:, 0:1]
    upper = frequency[:, 1:2]
    safe = jnp.where(offset == 0, 1.0, offset)
    ideal = (
        jnp.sin(2.0 * math.pi * upper * safe) - jnp.sin(2.0 * math.pi * lower * safe)
    ) / (math.pi * safe)
    ideal = jnp.where(offset == 0, 2.0 * (upper - lower), ideal)
    hamming = 0.54 - 0.46 * jnp.cos(2.0 * math.pi * sample_index / (TAPS - 1))
    taps = (ideal * hamming).astype(jnp.bfloat16)
    live = (tap >= 0) & (tap < TAPS)
    return jnp.where(live[None, :], taps, jnp.bfloat16(0)).astype(jnp.float32)


def strided(row, rows):
    wide = jnp.broadcast_to(row, (rows, row.shape[1]))
    return pltpu.roll(wide, 0, 1, stride=1, stride_axis=0)


def filter_kernel(taps_ref, out_ref):
    natural = lax.broadcasted_iota(jnp.int32, (128, 128), 0)
    order = lax.broadcasted_iota(jnp.int32, (128, 128), 1)
    time = ((order >> 2) & 3) * 32 + (order >> 4) * 4 + (order & 3)
    pick = (natural == time).astype(jnp.bfloat16)
    lane = lax.broadcasted_iota(jnp.int32, (128, 128), 1)
    row = lax.broadcasted_iota(jnp.int32, (128, 128), 0)
    for band in range(NB):
        before = None
        for part in range(3):
            piece = taps_ref[band : band + 1, part * 128 : (part + 1) * 128]
            rolled = strided(piece, 128)
            last = jnp.zeros_like(rolled) if before is None else before
            block = jnp.where(lane >= row, rolled, last).astype(jnp.bfloat16)
            ordered = jnp.dot(block, pick, preferred_element_type=jnp.float32)
            out_ref[band * 128 : (band + 1) * 128, part * 128 : (part + 1) * 128] = ordered.astype(jnp.bfloat16)
            before = rolled


def shuffle_kernel(x_ref, out_ref):
    group = lax.broadcasted_iota(jnp.int32, (16, 128), 1) >> 4
    for n in range(3):
        for tile in range(2):
            rows = []
            for b in range(8 * tile, 8 * tile + 8):
                parts = [x_ref[4 * b + q, n].astype(jnp.float32) for q in range(4)]
                rows.append(jnp.concatenate(parts, axis=0))
            for g in range(8):
                total = None
                for l in range(8):
                    turn = (16 * (l - g)) % 128
                    moved = rows[l] if turn == 0 else pltpu.roll(rows[l], turn, 1)
                    total = moved if total is None else jnp.where(group == l, moved, total)
                out_ref[g, 16 * n : 16 * n + 16, 128 * tile : 128 * tile + 128] = total.astype(jnp.bfloat16)


def whiten_kernel(filter_ref, x_ref, out_ref):
    lane = lax.broadcasted_iota(jnp.int32, (128, 256), 1)
    for n in range(3):
        here = jnp.concatenate([x_ref[g, 16 * n : 16 * n + 16, :] for g in range(8)], axis=0)
        wide = here.astype(jnp.float32)
        before = jnp.where(lane < 16, 0.0, pltpu.roll(wide, 16, 1)).astype(jnp.bfloat16)
        after = jnp.where(lane >= 240, 0.0, pltpu.roll(wide, 240, 1)).astype(jnp.bfloat16)
        window = jnp.concatenate([before, here, after], axis=0)
        total = None
        for band in range(NB):
            banded = jnp.dot(
                filter_ref[band * 128 : (band + 1) * 128, :], window, preferred_element_type=jnp.float32
            )
            power = jnp.sum(banded * banded, axis=0, keepdims=True)
            power = jnp.broadcast_to(power, (8, 256))
            for turn in (128, 64, 32, 16):
                power = power + pltpu.roll(power, turn, 1)
            scale = lax.rsqrt(power[0:1] * (1.0 / SAMPLES) + 1e-06)
            term = banded * scale
            total = term if total is None else total + term
        turned = jnp.concatenate([total[:, :128].T, total[:, 128:].T], axis=0)
        out_ref[256 * n : 256 * n + 256, :] = turned.astype(jnp.bfloat16)


def correlate_kernel(place_ref, left_ref, own_ref, right_ref, out_ref, rec, src, lhs, toe, res_a, res_b):
    zeros = jnp.zeros((128, 128), jnp.float32)
    for k in range(PMAX + 1):
        rec[pl.ds(k * 512, 128), :] = zeros
        rec[pl.ds(k * 512 + 384, 128), :] = zeros
        if k == PMAX:
            rec[pl.ds(k * 512 + 128, 128), :] = zeros
            rec[pl.ds(k * 512 + 256, 128), :] = zeros
            continue
        place = place_ref[k]
        row = pl.multiple_of(place_ref[16 + k], 256)

        @pl.when(place == -1)
        def _():
            rec[pl.ds(k * 512 + 128, 128), :] = zeros
            rec[pl.ds(k * 512 + 256, 128), :] = zeros

        for side, ref in enumerate((left_ref, own_ref, right_ref)):

            @pl.when(place == side)
            def _():
                rec[pl.ds(k * 512 + 128, 256), :] = ref[pl.ds(row, 256), :].astype(jnp.float32)

    src[...] = own_ref[256:512, :].astype(jnp.float32)
    zero_tile = jnp.zeros((128, 128), jnp.bfloat16)
    toe[128:256, 0:128] = zero_tile
    toe[0:128, 17 * 128 : 18 * 128] = zero_tile
    lane = lax.broadcasted_iota(jnp.int32, (128, 128), 1)
    line = lax.broadcasted_iota(jnp.int32, (128, 128), 0)
    lag_scale = 1.0 / (NB * math.sqrt(SAMPLES))

    def channel(c, carry):
        before = jnp.zeros((128, 128), jnp.float32)
        for b in range(17):
            if b < 16:
                rolled = strided(src[pl.ds(b * 16 + c, 1), :], 128)
            else:
                rolled = jnp.zeros((128, 128), jnp.float32)
            tile = jnp.where(lane >= line, rolled, before).astype(jnp.bfloat16)
            toe[0:128, 128 * b : 128 * b + 128] = tile
            toe[128:256, 128 * b + 128 : 128 * b + 256] = tile
            before = rolled
        for b in range(18):
            for pair in range(5):
                parts = [
                    rec[pl.ds((k * 32 + b) * 16 + c, 8, stride=32), :] for k in (2 * pair, 2 * pair + 1)
                ]
                lhs[16 * pair : 16 * pair + 16, 128 * b : 128 * b + 128] = jnp.concatenate(parts, axis=0).astype(
                    jnp.bfloat16
                )
        found = lax.dot_general(
            lhs[...], toe[...], (((1,), (1,)), ((), ())), preferred_element_type=jnp.float32
        )
        for k in range(PMAX):
            piece = found[8 * k : 8 * k + 8, :] * lag_scale
            res_a[pl.ds(k * 128 + c, 8, stride=16), :] = piece[:, :128]
            res_b[pl.ds(k * 128 + c, 8, stride=16), :] = piece[:, 128:]
        return carry

    lax.fori_loop(0, 16, channel, 0)
    for k in range(PMAX):
        parts = []
        for m in range(8):
            parts.append(res_a[k * 128 + 16 * m : k * 128 + 16 * m + 16, :])
            parts.append(res_b[k * 128 + 16 * m : k * 128 + 16 * m + 16, :])
        out_ref[k] = jnp.concatenate(parts, axis=1)[:, SHIFT : SHIFT + LAGS]


def call(kernel, out, args, scalars=0, scratch=(), flops=0):
    vmem = pl.BlockSpec(memory_space=pltpu.VMEM)
    smem = pl.BlockSpec(memory_space=pltpu.SMEM)
    size = sum(math.prod(a.shape) * a.dtype.itemsize for a in args) + math.prod(out.shape) * out.dtype.itemsize
    return pl.pallas_call(
        kernel,
        out_shape=out,
        in_specs=[smem] * scalars + [vmem] * (len(args) - scalars),
        out_specs=vmem,
        scratch_shapes=list(scratch),
        compiler_params=pltpu.CompilerParams(vmem_limit_bytes=VMEM_LIMIT),
        cost_estimate=pl.CostEstimate(flops=flops, bytes_accessed=size, transcendentals=0),
    )(*args)


def on_device(records, band_edges, receiver_block, slot_count):
    bf16 = jnp.bfloat16
    mine = records.reshape(4, 64, 128).transpose(1, 0, 2)
    sent = jnp.stack([jnp.roll(mine, 3, 0), mine, jnp.roll(mine, -3, 0)], axis=1)
    got = lax.all_to_all(sent, "tm", 0, 0, tiled=True)
    filters = call(
        filter_kernel, jax.ShapeDtypeStruct((512, 384), bf16), (taps_row(band_edges),), flops=2 * 512 * 384 * 128
    )
    shuffled = call(shuffle_kernel, jax.ShapeDtypeStruct((8, 48, 256), bf16), (got,))
    rows = lax.all_to_all(shuffled, "grp", 0, 0, tiled=True)
    own = call(
        whiten_kernel, jax.ShapeDtypeStruct((768, 128), bf16), (filters, rows), flops=2 * 3 * 512 * 384 * 256
    )
    size = lax.axis_size("tm")
    left = lax.ppermute(own, "tm", [(i, (i + 1) % size) for i in range(size)])
    right = lax.ppermute(own, "tm", [(i, (i - 1) % size) for i in range(size)])
    position = jnp.clip(receiver_block[0] - lax.axis_index("tm") + R, 0, 2 * R)
    live = jnp.arange(PMAX) < slot_count[0]
    places = jnp.concatenate(
        [
            jnp.where(live, position % 3, -1),
            jnp.zeros((16 - PMAX,), jnp.int32),
            256 * (position // 3),
            jnp.zeros((16 - PMAX,), jnp.int32),
        ]
    ).astype(jnp.int32)
    return call(
        correlate_kernel,
        jax.ShapeDtypeStruct((PMAX, 16, LAGS), jnp.float32),
        (places, left, own, right),
        scalars=1,
        scratch=[
            pltpu.VMEM(((PMAX + 1) * 512, 128), jnp.float32),
            pltpu.VMEM((256, 128), jnp.float32),
            pltpu.VMEM((80, 2304), bf16),
            pltpu.VMEM((256, 2304), bf16),
            pltpu.VMEM((PMAX * 128, 128), jnp.float32),
            pltpu.VMEM((PMAX * 128, 128), jnp.float32),
        ],
        flops=2 * 16 * 80 * 2304 * 256,
    )


def solution(mesh):
    return jax.shard_map(
        on_device,
        mesh=mesh,
        in_specs=(P(("tm", "grp"), None), P(), P("tm", None), P("tm")),
        out_specs=P("tm", "grp", None),
        check_vma=False,
    )
```

profile of v0, /device:TPU:1, one launch (start us, length us, event | category | flops | bytes accessed | tf_op | source)
XLA Modules:
  0.0 85.2 jit_solution(306228749609680168)
XLA Ops:
  0.0 0.0 copy-start
  0.0 0.7 fusion.9
  0.7 1.0 %fusion.10 = (bf16[61,4,128]{2,1,0:T(4,128)(2,1)S(1)}, bf16[61,4,128]{2,1,0:T(4,128)(2,1)S(1)}) fusion(bf16[64,4,128]{2,1,0:T(4,128)(2,1)} %bitcast.37), kind=kLoop, calls=%fused_computation.27 | loop fusion | bytes 249856 | tf_op jit(solution)/shard_map/jit(_roll_static)/slice | solution.py:191
  1.7 0.1 maximum_bitcast_fusion
  1.8 1.7 %pad_maximum_fusion = bf16[64,3,4,128]{3,2,1,0:T(4,128)(2,1)} fusion(bf16[64,1,4,128]{3,2,1,0:T(4,128)(2,1)S(1)} %get-tuple-element.19, bf16[64,1,4,128]{3,2,1,0:T(4,128)(2,1)} %bitcast.38, bf16[64,1,4,128]{3,2,1,0:T(4,128)(2,1)S(1)} %get-tuple-element.18), kind=kLoop, calls=%fused_computation | loop fusion | flops 196608 | bytes 393216 | tf_op jit(solution)/shard_map/stack | solution.py:191
  3.4 19.3 %all-to-all-start = ((bf16[64,3,4,128]{3,2,1,0:T(4,128)(2,1)}), bf16[64,3,4,128]{3,2,1,0:T(4,128)(2,1)S(1)}, u32[]{:S(2)}, u32[]{:S(2)}) async-start(bf16[64,3,4,128]{3,2,1,0:T(4,128)(2,1)} %pad_maximum_fusion), calls=%async_computation | async-start | bytes 393216 | tf_op jit(solution)/shard_map/all_to_all | solution.py:192
  22.7 0.0 copy-start.1
  23.5 0.0 copy-done
  23.5 15.9 %all-to-all-done.x_ref = bf16[64,3,4,128]{3,2,1,0:T(4,128)(2,1)S(1)} async-done(((bf16[64,3,4,128]{3,2,1,0:T(4,128)(2,1)}), bf16[64,3,4,128]{3,2,1,0:T(4,128)(2,1)S(1)}, u32[]{:S(2)}, u32[]{:S(2)}) %all-to-all-start) | async-done | bytes 196640 | tf_op jit(solution)/shard_map/all_to_all | solution.py:192
  39.4 1.1 %shard_map.47 = bf16[8,48,256]{2,1,0:T(8,128)(2,1)} custom-call(bf16[64,3,4,128]{3,2,1,0:T(4,128)(2,1)S(1)} %all-to-all-done.x_ref), custom_call_target="tpu_custom_call" | custom-call | bytes 393216 | tf_op jit(solution)/shard_map/pallas_call | solution.py:177
  40.5 6.8 %all-to-all-start.1 = ((bf16[8,48,256]{2,1,0:T(8,128)(2,1)}), bf16[8,48,256]{2,1,0:T(8,128)(2,1)S(1)}, u32[]{:S(2)}, u32[]{:S(2)}) async-start(bf16[8,48,256]{2,1,0:T(8,128)(2,1)} %shard_map.47), calls=%async_computation.1 | async-start | bytes 393216 | tf_op jit(solution)/shard_map/all_to_all | solution.py:197
  47.3 0.2 fusion.1.taps_ref
  47.5 0.3 shard_map.46.filter_ref
  47.8 5.4 %all-to-all-done.1.x_ref = bf16[8,48,256]{2,1,0:T(8,128)(2,1)S(1)} async-done(((bf16[8,48,256]{2,1,0:T(8,128)(2,1)}), bf16[8,48,256]{2,1,0:T(8,128)(2,1)S(1)}, u32[]{:S(2)}, u32[]{:S(2)}) %all-to-all-start.1) | async-done | bytes 196640 | tf_op jit(solution)/shard_map/all_to_all | solution.py:197
  53.2 1.1 %shard_map.48.own_ref = bf16[768,128]{1,0:T(8,128)(2,1)S(1)} custom-call(bf16[512,384]{1,0:T(8,128)(2,1)S(1)} %shard_map.46.filter_ref, bf16[8,48,256]{2,1,0:T(8,128)(2,1)S(1)} %all-to-all-done.1.x_ref), custom_call_target="tpu_custom_call" | custom-call | flops 301989888 | bytes 786432 | tf_op jit(solution)/shard_map/pallas_call | solution.py:177
  54.3 3.9 %collective-permute-start.1 = (bf16[768,128]{1,0:T(8,128)(2,1)S(1)}, bf16[768,128]{1,0:T(8,128)(2,1)S(1)}, u32[]{:S(2)}, u32[]{:S(2)}) collective-permute-start(bf16[768,128]{1,0:T(8,128)(2,1)S(1)} %shard_map.48.own_ref), channel_id=1, source_target_pairs={{0,504},{8,0},{16,8},{24,16},{32,24},{40,32},{48,40},{56,48},{64,5... | collective-permute-start | bytes 589832 | tf_op jit(solution)/shard_map/ppermute | solution.py:203
  58.2 1.9 %collective-permute-start = (bf16[768,128]{1,0:T(8,128)(2,1)S(1)}, bf16[768,128]{1,0:T(8,128)(2,1)S(1)}, u32[]{:S(2)}, u32[]{:S(2)}) collective-permute-start(bf16[768,128]{1,0:T(8,128)(2,1)S(1)} %shard_map.48.own_ref), channel_id=1, source_target_pairs={{0,8},{8,16},{16,24},{24,32},{32,40},{40,48},{48,56},{56,64},{64,7... | collective-permute-start | bytes 589832 | tf_op jit(solution)/shard_map/ppermute | solution.py:202
  60.1 0.0 copy-done.1
  60.2 0.1 pad_add_fusion.place_ref
  60.2 1.4 %collective-permute-done.1.right_ref = bf16[768,128]{1,0:T(8,128)(2,1)S(1)} collective-permute-done((bf16[768,128]{1,0:T(8,128)(2,1)S(1)}, bf16[768,128]{1,0:T(8,128)(2,1)S(1)}, u32[]{:S(2)}, u32[]{:S(2)}) %collective-permute-start.1) | collective-permute-done | bytes 196640 | tf_op jit(solution)/shard_map/ppermute | solution.py:203
  61.6 6.9 %collective-permute-done.left_ref = bf16[768,128]{1,0:T(8,128)(2,1)S(1)} collective-permute-done((bf16[768,128]{1,0:T(8,128)(2,1)S(1)}, bf16[768,128]{1,0:T(8,128)(2,1)S(1)}, u32[]{:S(2)}, u32[]{:S(2)}) %collective-permute-start) | collective-permute-done | bytes 196640 | tf_op jit(solution)/shard_map/ppermute | solution.py:202
  68.6 16.7 %shard_map.49 = f32[9,16,2001]{2,1,0:T(8,128)} custom-call(s32[32]{0:T(128)S(1)} %pad_add_fusion.place_ref, bf16[768,128]{1,0:T(8,128)(2,1)S(1)} %collective-permute-done.left_ref, bf16[768,128]{1,0:T(8,128)(2,1)S(1)} %shard_map.48.own_ref, bf16[768,128]{1,0:T(8,128)(2,1)S(1)} %collective-permute-done.1.right_ref), custom_call_target="tpu_custom_call" | custom-call | flops 1509949440 | bytes 1742528 | tf_op jit(solution)/shard_map/pallas_call | solution.py:177
  (7 shorter events, 0.1 us)
Async XLA Ops:
  0.0 23.5 %copy-start = (s32[4,2]{0,1:T(2,128)S(1)}, s32[4,2]{0,1:T(2,128)}, u32[]{:S(2)}) copy-start(s32[4,2]{0,1:T(2,128)} %param.5) | copy-start | bytes 100
  3.4 35.9 %all-to-all-start = ((bf16[64,3,4,128]{3,2,1,0:T(4,128)(2,1)}), bf16[64,3,4,128]{3,2,1,0:T(4,128)(2,1)S(1)}, u32[]{:S(2)}, u32[]{:S(2)}) async-start(bf16[64,3,4,128]{3,2,1,0:T(4,128)(2,1)} %pad_maximum_fusion), calls=%async_computation | async-start | bytes 393216 | tf_op jit(solution)/shard_map/all_to_all | solution.py:192
  22.7 37.4 %copy-start.1 = (s32[1,9]{1,0:T(1,128)S(1)}, s32[1,9]{1,0:T(1,128)}, u32[]{:S(2)}) copy-start(s32[1,9]{1,0:T(1,128)} %param.6) | copy-start | bytes 112
  40.5 12.7 %all-to-all-start.1 = ((bf16[8,48,256]{2,1,0:T(8,128)(2,1)}), bf16[8,48,256]{2,1,0:T(8,128)(2,1)S(1)}, u32[]{:S(2)}, u32[]{:S(2)}) async-start(bf16[8,48,256]{2,1,0:T(8,128)(2,1)} %shard_map.47), calls=%async_computation.1 | async-start | bytes 393216 | tf_op jit(solution)/shard_map/all_to_all | solution.py:197
  54.3 7.3 %collective-permute-start.1 = (bf16[768,128]{1,0:T(8,128)(2,1)S(1)}, bf16[768,128]{1,0:T(8,128)(2,1)S(1)}, u32[]{:S(2)}, u32[]{:S(2)}) collective-permute-start(bf16[768,128]{1,0:T(8,128)(2,1)S(1)} %shard_map.48.own_ref), channel_id=1, source_target_pairs={{0,504},{8,0},{16,8},{24,16},{32,24},{40,32},{48,40},{56,48},{64,5... | collective-permute-start | bytes 589832 | tf_op jit(solution)/shard_map/ppermute | solution.py:203
  58.2 10.4 %collective-permute-start = (bf16[768,128]{1,0:T(8,128)(2,1)S(1)}, bf16[768,128]{1,0:T(8,128)(2,1)S(1)}, u32[]{:S(2)}, u32[]{:S(2)}) collective-permute-start(bf16[768,128]{1,0:T(8,128)(2,1)S(1)} %shard_map.48.own_ref), channel_id=1, source_target_pairs={{0,8},{8,16},{16,24},{24,32},{32,40},{40,48},{48,56},{56,64},{64,7... | collective-permute-start | bytes 589832 | tf_op jit(solution)/shard_map/ppermute | solution.py:202
where the time goes:
time: 85.7 us; the launch traced here: 85.2 us
  starting transfers between devices  31.9 us (37%)
  waiting for transfers between devices  29.6 us (35%)
  Pallas kernels  19.1 us (22%)
  other arithmetic  2.11 us (2%)
  local copies, waits for them, and re-layouts  1.68 us (2%)
    all_to_all x1, starting transfers between devices, on_device(): got = lax.all_to_all(sent, 'tm', 0, 0, tiled=True)  19.3 us
    pallas_call x4, Pallas kernels, call(): pl.pallas_call(kernel, out_shape=out, in_specs=[smem] * scalars + [vmem]...  19.1 us
    all_to_all x1, waiting for transfers between devices, on_device(): got = lax.all_to_all(sent, 'tm', 0, 0, tiled=True)  15.9 us
    ppermute x1, waiting for transfers between devices, on_device(): left = lax.ppermute(own, 'tm', [(i, (i + 1) % size) for i in range(size)])  6.94 us
    all_to_all x1, starting transfers between devices, on_device(): rows = lax.all_to_all(shuffled, 'grp', 0, 0, tiled=True)  6.83 us
    all_to_all x1, waiting for transfers between devices, on_device(): rows = lax.all_to_all(shuffled, 'grp', 0, 0, tiled=True)  5.39 us
    ppermute x1, starting transfers between devices, on_device(): right = lax.ppermute(own, 'tm', [(i, (i - 1) % size) for i in range(size)])  3.91 us
    ppermute x1, starting transfers between devices, on_device(): left = lax.ppermute(own, 'tm', [(i, (i + 1) % size) for i in range(size)])  1.92 us
  transfers between devices with their start and end apart: 4, of which 4 were waited for; matrix products, arithmetic and copies ran while one was open for 0% of the time, Pallas kernels for 0%

commit v1 on v0

--- a/solution.py
+++ b/solution.py
@@ -16,7 +16,7 @@
 LAGS = 2001
 SAMPLES = 2048
 SHIFT = 24
-VMEM_LIMIT = 48 * 1024 * 1024
+VMEM_LIMIT = 32 * 1024 * 1024
 
 
 def taps_row(band_edges):
@@ -102,7 +102,40 @@
         out_ref[256 * n : 256 * n + 256, :] = turned.astype(jnp.bfloat16)
 
 
-def correlate_kernel(place_ref, left_ref, own_ref, right_ref, out_ref, rec, src, lhs, toe, res_a, res_b):
+def spread_kernel(x_ref, out_ref):
+    for o in range(64):
+        block = x_ref[:, 128 * o : 128 * o + 128]
+        out_ref[(o + 3) % 64, 0] = block
+        out_ref[o, 1] = block
+        out_ref[(o - 3) % 64, 2] = block
+
+
+def toeplitz_kernel(own_ref, out_ref, src):
+    line = lax.broadcasted_iota(jnp.int32, (128, 128), 0)
+    lane = lax.broadcasted_iota(jnp.int32, (128, 128), 1)
+    turn = (line + lane == 127).astype(jnp.bfloat16)
+    src[...] = jnp.dot(own_ref[256:512, :], turn, preferred_element_type=jnp.float32)
+    zero_tile = jnp.zeros((128, 128), jnp.bfloat16)
+
+    def channel(c, carry):
+        before = jnp.zeros((128, 128), jnp.float32)
+        out_ref[c, 0:128, :] = zero_tile
+        for e in range(17):
+            if e < 16:
+                wide = jnp.broadcast_to(src[pl.ds(e * 16 + c, 1), :], (128, 128))
+                rolled = pltpu.roll(wide, 1, 1, stride=1, stride_axis=0)
+            else:
+                rolled = jnp.zeros((128, 128), jnp.float32)
+            tile = jnp.where(lane <= line, rolled, before).astype(jnp.bfloat16)
+            out_ref[c, 128 * e + 128 : 128 * e + 256, :] = tile
+            before = rolled
+        out_ref[c, 18 * 128 : 19 * 128, :] = zero_tile
+        return carry
+
+    lax.fori_loop(0, 16, channel, 0)
+
+
+def correlate_kernel(place_ref, toe_ref, left_ref, own_ref, right_ref, out_ref, rec, lhs_0, lhs_1, res_a, res_b):
     zeros = jnp.zeros((128, 128), jnp.float32)
     for k in range(PMAX + 1):
         rec[pl.ds(k * 512, 128), :] = zeros
@@ -125,25 +158,9 @@
             def _():
                 rec[pl.ds(k * 512 + 128, 256), :] = ref[pl.ds(row, 256), :].astype(jnp.float32)
 
-    src[...] = own_ref[256:512, :].astype(jnp.float32)
-    zero_tile = jnp.zeros((128, 128), jnp.bfloat16)
-    toe[128:256, 0:128] = zero_tile
-    toe[0:128, 17 * 128 : 18 * 128] = zero_tile
-    lane = lax.broadcasted_iota(jnp.int32, (128, 128), 1)
-    line = lax.broadcasted_iota(jnp.int32, (128, 128), 0)
     lag_scale = 1.0 / (NB * math.sqrt(SAMPLES))
 
-    def channel(c, carry):
-        before = jnp.zeros((128, 128), jnp.float32)
-        for b in range(17):
-            if b < 16:
-                rolled = strided(src[pl.ds(b * 16 + c, 1), :], 128)
-            else:
-                rolled = jnp.zeros((128, 128), jnp.float32)
-            tile = jnp.where(lane >= line, rolled, before).astype(jnp.bfloat16)
-            toe[0:128, 128 * b : 128 * b + 128] = tile
-            toe[128:256, 128 * b + 128 : 128 * b + 256] = tile
-            before = rolled
+    def fill(lhs, c):
         for b in range(18):
             for pair in range(5):
                 parts = [
@@ -152,16 +169,23 @@
                 lhs[16 * pair : 16 * pair + 16, 128 * b : 128 * b + 128] = jnp.concatenate(parts, axis=0).astype(
                     jnp.bfloat16
                 )
-        found = lax.dot_general(
-            lhs[...], toe[...], (((1,), (1,)), ((), ())), preferred_element_type=jnp.float32
-        )
+
+    def work(lhs, c):
+        matrix = jnp.concatenate([toe_ref[c, 128:2432, :], toe_ref[c, 0:2304, :]], axis=1)
+        found = jnp.dot(lhs[...], matrix, preferred_element_type=jnp.float32)
         for k in range(PMAX):
             piece = found[8 * k : 8 * k + 8, :] * lag_scale
             res_a[pl.ds(k * 128 + c, 8, stride=16), :] = piece[:, :128]
             res_b[pl.ds(k * 128 + c, 8, stride=16), :] = piece[:, 128:]
+
+    def two(i, carry):
+        fill(lhs_0, 2 * i)
+        fill(lhs_1, 2 * i + 1)
+        work(lhs_0, 2 * i)
+        work(lhs_1, 2 * i + 1)
         return carry
 
-    lax.fori_loop(0, 16, channel, 0)
+    lax.fori_loop(0, 8, two, 0)
     for k in range(PMAX):
         parts = []
         for m in range(8):
@@ -187,8 +211,7 @@
 
 def on_device(records, band_edges, receiver_block, slot_count):
     bf16 = jnp.bfloat16
-    mine = records.reshape(4, 64, 128).transpose(1, 0, 2)
-    sent = jnp.stack([jnp.roll(mine, 3, 0), mine, jnp.roll(mine, -3, 0)], axis=1)
+    sent = call(spread_kernel, jax.ShapeDtypeStruct((64, 3, 4, 128), bf16), (records,))
     got = lax.all_to_all(sent, "tm", 0, 0, tiled=True)
     filters = call(
         filter_kernel, jax.ShapeDtypeStruct((512, 384), bf16), (taps_row(band_edges),), flops=2 * 512 * 384 * 128
@@ -201,6 +224,13 @@
     size = lax.axis_size("tm")
     left = lax.ppermute(own, "tm", [(i, (i + 1) % size) for i in range(size)])
     right = lax.ppermute(own, "tm", [(i, (i - 1) % size) for i in range(size)])
+    toe = call(
+        toeplitz_kernel,
+        jax.ShapeDtypeStruct((16, 2432, 128), bf16),
+        (own,),
+        scratch=[pltpu.VMEM((256, 128), jnp.float32)],
+        flops=2 * 16 * 2432 * 128 * 256,
+    )
     position = jnp.clip(receiver_block[0] - lax.axis_index("tm") + R, 0, 2 * R)
     live = jnp.arange(PMAX) < slot_count[0]
     places = jnp.concatenate(
@@ -214,13 +244,12 @@
     return call(
         correlate_kernel,
         jax.ShapeDtypeStruct((PMAX, 16, LAGS), jnp.float32),
-        (places, left, own, right),
+        (places, toe, left, own, right),
         scalars=1,
         scratch=[
             pltpu.VMEM(((PMAX + 1) * 512, 128), jnp.float32),
-            pltpu.VMEM((256, 128), jnp.float32),
             pltpu.VMEM((80, 2304), bf16),
-            pltpu.VMEM((256, 2304), bf16),
+            pltpu.VMEM((80, 2304), bf16),
             pltpu.VMEM((PMAX * 128, 128), jnp.float32),
             pltpu.VMEM((PMAX * 128, 128), jnp.float32),
         ],

time: 85.7 us -> 79.2 us (0.924)
  waiting for transfers between devices: 29.6 us -> 24.7 us
    ppermute x1, waiting for transfers between devices: 6.94 us -> 4.86 us  [on_device(): left = lax.ppermute(own, 'tm', [(i, (i + 1) % size) for i in range(size)])]
    another operation x2 -> x0, other arithmetic: 1.77 us -> none  [on_device(): jnp.stack([jnp.roll(mine, 3, 0), mine, jnp.roll(mine, -3, 0)], axis=1)]
    slice x2 -> x0, local copies, waits for them, and re-layouts: 1.67 us -> none  [on_device(): jnp.roll(mine, 3, 0)]
    ppermute x1, waiting for transfers between devices: 1.38 us -> 0.01 us  [on_device(): right = lax.ppermute(own, 'tm', [(i, (i - 1) % size) for i in range(size)])]
    pallas_call x4 -> x6, Pallas kernels: 19.1 us -> 19 us  [call(): pl.pallas_call(kernel, out_shape=out, in_specs=[smem] * scalars + [vmem]...]
  transfers between devices with their start and end apart: 4 -> 4, of which waited for: 4 -> 3; matrix products, arithmetic and copies ran while one was open for 0% -> 2% of each run, Pallas kernels for 0% -> 5%
where the time goes in v1:
time: 79.2 us; the launch traced here: 78.9 us
  starting transfers between devices  31.9 us (40%)
  waiting for transfers between devices  24.7 us (31%)
  Pallas kernels  19 us (24%)
  other arithmetic  1.68 us (2%)
  local copies, waits for them, and re-layouts  0.84 us (1%)
    all_to_all x1, starting transfers between devices, on_device(): got = lax.all_to_all(sent, 'tm', 0, 0, tiled=True)  19.3 us
    pallas_call x6, Pallas kernels, call(): pl.pallas_call(kernel, out_shape=out, in_specs=[smem] * scalars + [vmem]...  19 us
    all_to_all x1, waiting for transfers between devices, on_device(): got = lax.all_to_all(sent, 'tm', 0, 0, tiled=True)  15 us
    all_to_all x1, starting transfers between devices, on_device(): rows = lax.all_to_all(shuffled, 'grp', 0, 0, tiled=True)  6.83 us
    ppermute x1, waiting for transfers between devices, on_device(): left = lax.ppermute(own, 'tm', [(i, (i + 1) % size) for i in range(size)])  4.86 us
    all_to_all x1, waiting for transfers between devices, on_device(): rows = lax.all_to_all(shuffled, 'grp', 0, 0, tiled=True)  4.8 us
    ppermute x1, starting transfers between devices, on_device(): right = lax.ppermute(own, 'tm', [(i, (i - 1) % size) for i in range(size)])  3.91 us
    ppermute x1, starting transfers between devices, on_device(): left = lax.ppermute(own, 'tm', [(i, (i + 1) % size) for i in range(size)])  1.92 us
  transfers between devices with their start and end apart: 4, of which 3 were waited for; matrix products, arithmetic and copies ran while one was open for 2% of the time, Pallas kernels for 5%

profile of v1, /device:TPU:1, one launch (start us, length us, event | category | flops | bytes accessed | tf_op | source)
XLA Modules:
  0.0 78.9 jit_solution(3428473743998038305)
XLA Ops:
  0.0 0.0 copy-start
  0.0 0.8 %copy-done = bf16[4,8192]{1,0:T(4,128)(2,1)S(1)} copy-done((bf16[4,8192]{1,0:T(4,128)(2,1)S(1)}, bf16[4,8192]{1,0:T(4,128)(2,1)}, u32[]{:S(2)}) %copy-start) | copy-done | bytes 65560
  0.8 0.7 shard_map.47
  1.6 19.3 %all-to-all-start = ((bf16[64,3,4,128]{3,2,1,0:T(4,128)(2,1)}), bf16[64,3,4,128]{3,2,1,0:T(4,128)(2,1)S(1)}, u32[]{:S(2)}, u32[]{:S(2)}) async-start(bf16[64,3,4,128]{3,2,1,0:T(4,128)(2,1)} %shard_map.47), calls=%async_computation | async-start | bytes 393216 | tf_op jit(solution)/shard_map/all_to_all | solution.py:215
  21.6 0.7 convert_multiply_fusion
  22.3 0.2 fusion.1.taps_ref
  22.5 15.0 %all-to-all-done.x_ref = bf16[64,3,4,128]{3,2,1,0:T(4,128)(2,1)S(1)} async-done(((bf16[64,3,4,128]{3,2,1,0:T(4,128)(2,1)}), bf16[64,3,4,128]{3,2,1,0:T(4,128)(2,1)S(1)}, u32[]{:S(2)}, u32[]{:S(2)}) %all-to-all-start) | async-done | bytes 196640 | tf_op jit(solution)/shard_map/all_to_all | solution.py:215
  37.5 1.1 %shard_map.48 = bf16[8,48,256]{2,1,0:T(8,128)(2,1)} custom-call(bf16[64,3,4,128]{3,2,1,0:T(4,128)(2,1)S(1)} %all-to-all-done.x_ref), custom_call_target="tpu_custom_call" | custom-call | bytes 393216 | tf_op jit(solution)/shard_map/pallas_call | solution.py:201
  38.6 6.8 %all-to-all-start.1 = ((bf16[8,48,256]{2,1,0:T(8,128)(2,1)}), bf16[8,48,256]{2,1,0:T(8,128)(2,1)S(1)}, u32[]{:S(2)}, u32[]{:S(2)}) async-start(bf16[8,48,256]{2,1,0:T(8,128)(2,1)} %shard_map.48), calls=%async_computation.1 | async-start | bytes 393216 | tf_op jit(solution)/shard_map/all_to_all | solution.py:220
  45.4 0.7 compare_select_fusion
  46.1 0.3 shard_map.46.filter_ref
  46.4 0.1 pad_add_fusion.place_ref
  46.5 4.8 %all-to-all-done.1.x_ref = bf16[8,48,256]{2,1,0:T(8,128)(2,1)S(1)} async-done(((bf16[8,48,256]{2,1,0:T(8,128)(2,1)}), bf16[8,48,256]{2,1,0:T(8,128)(2,1)S(1)}, u32[]{:S(2)}, u32[]{:S(2)}) %all-to-all-start.1) | async-done | bytes 196640 | tf_op jit(solution)/shard_map/all_to_all | solution.py:220
  51.3 1.1 %shard_map.49.own_ref = bf16[768,128]{1,0:T(8,128)(2,1)S(1)} custom-call(bf16[512,384]{1,0:T(8,128)(2,1)S(1)} %shard_map.46.filter_ref, bf16[8,48,256]{2,1,0:T(8,128)(2,1)S(1)} %all-to-all-done.1.x_ref), custom_call_target="tpu_custom_call" | custom-call | flops 301989888 | bytes 786432 | tf_op jit(solution)/shard_map/pallas_call | solution.py:201
  52.4 3.9 %collective-permute-start.1 = (bf16[768,128]{1,0:T(8,128)(2,1)S(1)}, bf16[768,128]{1,0:T(8,128)(2,1)S(1)}, u32[]{:S(2)}, u32[]{:S(2)}) collective-permute-start(bf16[768,128]{1,0:T(8,128)(2,1)S(1)} %shard_map.49.own_ref), channel_id=1, source_target_pairs={{0,504},{8,0},{16,8},{24,16},{32,24},{40,32},{48,40},{56,48},{64,5... | collective-permute-start | bytes 589832 | tf_op jit(solution)/shard_map/ppermute | solution.py:226
  56.3 1.9 %collective-permute-start = (bf16[768,128]{1,0:T(8,128)(2,1)S(1)}, bf16[768,128]{1,0:T(8,128)(2,1)S(1)}, u32[]{:S(2)}, u32[]{:S(2)}) collective-permute-start(bf16[768,128]{1,0:T(8,128)(2,1)S(1)} %shard_map.49.own_ref), channel_id=1, source_target_pairs={{0,8},{8,16},{16,24},{24,32},{32,40},{40,48},{48,56},{56,64},{64,7... | collective-permute-start | bytes 589832 | tf_op jit(solution)/shard_map/ppermute | solution.py:225
  58.2 3.6 %shard_map.50.toe_ref = bf16[16,2432,128]{2,1,0:T(8,128)(2,1)S(1)} custom-call(bf16[768,128]{1,0:T(8,128)(2,1)S(1)} %shard_map.49.own_ref), custom_call_target="tpu_custom_call" | custom-call | flops 2550136832 | bytes 10158080 | tf_op jit(solution)/shard_map/pallas_call | solution.py:201
  61.8 0.0 collective-permute-done.1.right_ref
  61.8 4.9 %collective-permute-done.left_ref = bf16[768,128]{1,0:T(8,128)(2,1)S(1)} collective-permute-done((bf16[768,128]{1,0:T(8,128)(2,1)S(1)}, bf16[768,128]{1,0:T(8,128)(2,1)S(1)}, u32[]{:S(2)}, u32[]{:S(2)}) %collective-permute-start) | collective-permute-done | bytes 196640 | tf_op jit(solution)/shard_map/ppermute | solution.py:225
  66.7 12.2 %shard_map.51 = f32[9,16,2001]{2,1,0:T(8,128)} custom-call(s32[32]{0:T(128)S(1)} %pad_add_fusion.place_ref, bf16[16,2432,128]{2,1,0:T(8,128)(2,1)S(1)} %shard_map.50.toe_ref, bf16[768,128]{1,0:T(8,128)(2,1)S(1)} %collective-permute-done.left_ref, bf16[768,128]{1,0:T(8,128)(2,1)S(1)} %shard_map.49.own_ref, bf16[768,128]{1,0:T(8,128)(2,1)S(1)} %collective-permute-done.1.right_ref), custom_call_target="tpu_custom_call" | custom-call | flops 1509949440 | bytes 11704000 | tf_op jit(solution)/shard_map/pallas_call | solution.py:201
  (5 shorter events, 0.1 us)
Async XLA Ops:
  0.0 0.8 %copy-start = (bf16[4,8192]{1,0:T(4,128)(2,1)S(1)}, bf16[4,8192]{1,0:T(4,128)(2,1)}, u32[]{:S(2)}) copy-start(bf16[4,8192]{1,0:T(4,128)(2,1)} %x_ref.1) | copy-start | bytes 196612
  1.6 35.9 %all-to-all-start = ((bf16[64,3,4,128]{3,2,1,0:T(4,128)(2,1)}), bf16[64,3,4,128]{3,2,1,0:T(4,128)(2,1)S(1)}, u32[]{:S(2)}, u32[]{:S(2)}) async-start(bf16[64,3,4,128]{3,2,1,0:T(4,128)(2,1)} %shard_map.47), calls=%async_computation | async-start | bytes 393216 | tf_op jit(solution)/shard_map/all_to_all | solution.py:215
  38.6 12.7 %all-to-all-start.1 = ((bf16[8,48,256]{2,1,0:T(8,128)(2,1)}), bf16[8,48,256]{2,1,0:T(8,128)(2,1)S(1)}, u32[]{:S(2)}, u32[]{:S(2)}) async-start(bf16[8,48,256]{2,1,0:T(8,128)(2,1)} %shard_map.48), calls=%async_computation.1 | async-start | bytes 393216 | tf_op jit(solution)/shard_map/all_to_all | solution.py:220
  52.4 9.4 %collective-permute-start.1 = (bf16[768,128]{1,0:T(8,128)(2,1)S(1)}, bf16[768,128]{1,0:T(8,128)(2,1)S(1)}, u32[]{:S(2)}, u32[]{:S(2)}) collective-permute-start(bf16[768,128]{1,0:T(8,128)(2,1)S(1)} %shard_map.49.own_ref), channel_id=1, source_target_pairs={{0,504},{8,0},{16,8},{24,16},{32,24},{40,32},{48,40},{56,48},{64,5... | collective-permute-start | bytes 589832 | tf_op jit(solution)/shard_map/ppermute | solution.py:226
  56.3 10.4 %collective-permute-start = (bf16[768,128]{1,0:T(8,128)(2,1)S(1)}, bf16[768,128]{1,0:T(8,128)(2,1)S(1)}, u32[]{:S(2)}, u32[]{:S(2)}) collective-permute-start(bf16[768,128]{1,0:T(8,128)(2,1)S(1)} %shard_map.49.own_ref), channel_id=1, source_target_pairs={{0,8},{8,16},{16,24},{24,32},{32,40},{40,48},{48,56},{56,64},{64,7... | collective-permute-start | bytes 589832 | tf_op jit(solution)/shard_map/ppermute | solution.py:225

commit v2 on v1

--- a/solution.py
+++ b/solution.py
@@ -80,6 +80,10 @@
 
 def whiten_kernel(filter_ref, x_ref, out_ref):
     lane = lax.broadcasted_iota(jnp.int32, (128, 256), 1)
+    row = lax.broadcasted_iota(jnp.int32, (256, 256), 0)
+    column = lax.broadcasted_iota(jnp.int32, (256, 256), 1)
+    wanted = (2 * (row & 7) + ((row >> 3) & 1)) * 16 + (row >> 4)
+    pick = (column == wanted).astype(jnp.bfloat16)
     for n in range(3):
         here = jnp.concatenate([x_ref[g, 16 * n : 16 * n + 16, :] for g in range(8)], axis=0)
         wide = here.astype(jnp.float32)
@@ -98,7 +102,9 @@
             scale = lax.rsqrt(power[0:1] * (1.0 / SAMPLES) + 1e-06)
             term = banded * scale
             total = term if total is None else total + term
-        turned = jnp.concatenate([total[:, :128].T, total[:, 128:].T], axis=0)
+        turned = lax.dot_general(
+            pick, total.astype(jnp.bfloat16), (((1,), (1,)), ((), ())), preferred_element_type=jnp.float32
+        )
         out_ref[256 * n : 256 * n + 256, :] = turned.astype(jnp.bfloat16)
 
 
@@ -122,7 +128,7 @@
         out_ref[c, 0:128, :] = zero_tile
         for e in range(17):
             if e < 16:
-                wide = jnp.broadcast_to(src[pl.ds(e * 16 + c, 1), :], (128, 128))
+                wide = jnp.broadcast_to(src[pl.ds(c * 16 + (e % 2) * 8 + e // 2, 1), :], (128, 128))
                 rolled = pltpu.roll(wide, 1, 1, stride=1, stride_axis=0)
             else:
                 rolled = jnp.zeros((128, 128), jnp.float32)
@@ -136,39 +142,38 @@
 
 
 def correlate_kernel(place_ref, toe_ref, left_ref, own_ref, right_ref, out_ref, rec, lhs_0, lhs_1, res_a, res_b):
-    zeros = jnp.zeros((128, 128), jnp.float32)
-    for k in range(PMAX + 1):
-        rec[pl.ds(k * 512, 128), :] = zeros
-        rec[pl.ds(k * 512 + 384, 128), :] = zeros
-        if k == PMAX:
-            rec[pl.ds(k * 512 + 128, 128), :] = zeros
-            rec[pl.ds(k * 512 + 256, 128), :] = zeros
-            continue
+    zeros = jnp.zeros((8, 128), jnp.float32)
+    for i in range(PMAX * 32 + 1):
+        rec[16 * i : 16 * i + 8, :] = zeros
+    for k in range(PMAX):
         place = place_ref[k]
         row = pl.multiple_of(place_ref[16 + k], 256)
 
         @pl.when(place == -1)
         def _():
-            rec[pl.ds(k * 512 + 128, 128), :] = zeros
-            rec[pl.ds(k * 512 + 256, 128), :] = zeros
+            for i in range(32):
+                rec[(k * 32 + i) * 16 + 8 : (k * 32 + i) * 16 + 16, :] = zeros
 
         for side, ref in enumerate((left_ref, own_ref, right_ref)):
 
             @pl.when(place == side)
             def _():
-                rec[pl.ds(k * 512 + 128, 256), :] = ref[pl.ds(row, 256), :].astype(jnp.float32)
+                rows = ref[pl.ds(row, 256), :].astype(jnp.float32)
+                for i in range(32):
+                    rec[(k * 32 + i) * 16 + 8 : (k * 32 + i) * 16 + 16, :] = rows[8 * i : 8 * i + 8, :]
 
     lag_scale = 1.0 / (NB * math.sqrt(SAMPLES))
 
     def fill(lhs, c):
+        first = pl.multiple_of(c * 32, 32)
         for b in range(18):
+            parts = []
+            for k in range(PMAX):
+                parts.append(rec[pl.ds(first + (k * 512 + (b % 2) * 16 + 4 + b // 2), 8), :])
+            parts.append(zeros)
             for pair in range(5):
-                parts = [
-                    rec[pl.ds((k * 32 + b) * 16 + c, 8, stride=32), :] for k in (2 * pair, 2 * pair + 1)
-                ]
-                lhs[16 * pair : 16 * pair + 16, 128 * b : 128 * b + 128] = jnp.concatenate(parts, axis=0).astype(
-                    jnp.bfloat16
-                )
+                both = jnp.concatenate(parts[2 * pair : 2 * pair + 2], axis=0).astype(jnp.bfloat16)
+                lhs[16 * pair : 16 * pair + 16, 128 * b : 128 * b + 128] = both
 
     def work(lhs, c):
         matrix = jnp.concatenate([toe_ref[c, 128:2432, :], toe_ref[c, 0:2304, :]], axis=1)
@@ -247,7 +252,7 @@
         (places, toe, left, own, right),
         scalars=1,
         scratch=[
-            pltpu.VMEM(((PMAX + 1) * 512, 128), jnp.float32),
+            pltpu.VMEM((PMAX * 512 + 8, 128), jnp.float32),
             pltpu.VMEM((80, 2304), bf16),
             pltpu.VMEM((80, 2304), bf16),
             pltpu.VMEM((PMAX * 128, 128), jnp.float32),

time: 79.2 us -> 75.2 us (0.949)
  Pallas kernels: 19 us -> 14.9 us
    pallas_call x6, Pallas kernels: 19 us -> 14.9 us  [call(): pl.pallas_call(kernel, out_shape=out, in_specs=[smem] * scalars + [vmem]...]
where the time goes in v2:
time: 75.2 us; the launch traced here: 74.8 us
  starting transfers between devices  31.9 us (42%)
  waiting for transfers between devices  24.7 us (33%)
  Pallas kernels  14.9 us (20%)
  other arithmetic  1.68 us (2%)
  local copies, waits for them, and re-layouts  0.84 us (1%)
    all_to_all x1, starting transfers between devices, on_device(): got = lax.all_to_all(sent, 'tm', 0, 0, tiled=True)  19.3 us
    all_to_all x1, waiting for transfers between devices, on_device(): got = lax.all_to_all(sent, 'tm', 0, 0, tiled=True)  15 us
    pallas_call x6, Pallas kernels, call(): pl.pallas_call(kernel, out_shape=out, in_specs=[smem] * scalars + [vmem]...  14.9 us
    all_to_all x1, starting transfers between devices, on_device(): rows = lax.all_to_all(shuffled, 'grp', 0, 0, tiled=True)  6.83 us
    ppermute x1, waiting for transfers between devices, on_device(): left = lax.ppermute(own, 'tm', [(i, (i + 1) % size) for i in range(size)])  4.86 us
    all_to_all x1, waiting for transfers between devices, on_device(): rows = lax.all_to_all(shuffled, 'grp', 0, 0, tiled=True)  4.8 us
    ppermute x1, starting transfers between devices, on_device(): right = lax.ppermute(own, 'tm', [(i, (i - 1) % size) for i in range(size)])  3.9 us
    ppermute x1, starting transfers between devices, on_device(): left = lax.ppermute(own, 'tm', [(i, (i + 1) % size) for i in range(size)])  1.92 us
  transfers between devices with their start and end apart: 4, of which 3 were waited for; matrix products, arithmetic and copies ran while one was open for 2% of the time, Pallas kernels for 5%

profile of v2, /device:TPU:1, one launch (start us, length us, event | category | flops | bytes accessed | tf_op | source)
XLA Modules:
  0.0 74.8 jit_solution(10301458252123393025)
XLA Ops:
  0.0 0.0 copy-start
  0.0 0.8 %copy-done = bf16[4,8192]{1,0:T(4,128)(2,1)S(1)} copy-done((bf16[4,8192]{1,0:T(4,128)(2,1)S(1)}, bf16[4,8192]{1,0:T(4,128)(2,1)}, u32[]{:S(2)}) %copy-start) | copy-done | bytes 65560
  0.8 0.7 shard_map.47
  1.6 19.3 %all-to-all-start = ((bf16[64,3,4,128]{3,2,1,0:T(4,128)(2,1)}), bf16[64,3,4,128]{3,2,1,0:T(4,128)(2,1)S(1)}, u32[]{:S(2)}, u32[]{:S(2)}) async-start(bf16[64,3,4,128]{3,2,1,0:T(4,128)(2,1)} %shard_map.47), calls=%async_computation | async-start | bytes 393216 | tf_op jit(solution)/shard_map/all_to_all | solution.py:220
  21.6 0.7 convert_multiply_fusion
  22.3 0.2 fusion.1.taps_ref
  22.5 15.0 %all-to-all-done.x_ref = bf16[64,3,4,128]{3,2,1,0:T(4,128)(2,1)S(1)} async-done(((bf16[64,3,4,128]{3,2,1,0:T(4,128)(2,1)}), bf16[64,3,4,128]{3,2,1,0:T(4,128)(2,1)S(1)}, u32[]{:S(2)}, u32[]{:S(2)}) %all-to-all-start) | async-done | bytes 196640 | tf_op jit(solution)/shard_map/all_to_all | solution.py:220
  37.5 1.1 %shard_map.48 = bf16[8,48,256]{2,1,0:T(8,128)(2,1)} custom-call(bf16[64,3,4,128]{3,2,1,0:T(4,128)(2,1)S(1)} %all-to-all-done.x_ref), custom_call_target="tpu_custom_call" | custom-call | bytes 393216 | tf_op jit(solution)/shard_map/pallas_call | solution.py:206
  38.6 6.8 %all-to-all-start.1 = ((bf16[8,48,256]{2,1,0:T(8,128)(2,1)}), bf16[8,48,256]{2,1,0:T(8,128)(2,1)S(1)}, u32[]{:S(2)}, u32[]{:S(2)}) async-start(bf16[8,48,256]{2,1,0:T(8,128)(2,1)} %shard_map.48), calls=%async_computation.1 | async-start | bytes 393216 | tf_op jit(solution)/shard_map/all_to_all | solution.py:225
  45.4 0.7 compare_select_fusion
  46.1 0.3 shard_map.46.filter_ref
  46.4 0.1 pad_add_fusion.place_ref
  46.5 4.8 %all-to-all-done.1.x_ref = bf16[8,48,256]{2,1,0:T(8,128)(2,1)S(1)} async-done(((bf16[8,48,256]{2,1,0:T(8,128)(2,1)}), bf16[8,48,256]{2,1,0:T(8,128)(2,1)S(1)}, u32[]{:S(2)}, u32[]{:S(2)}) %all-to-all-start.1) | async-done | bytes 196640 | tf_op jit(solution)/shard_map/all_to_all | solution.py:225
  51.3 2.1 %shard_map.49.own_ref = bf16[768,128]{1,0:T(8,128)(2,1)S(1)} custom-call(bf16[512,384]{1,0:T(8,128)(2,1)S(1)} %shard_map.46.filter_ref, bf16[8,48,256]{2,1,0:T(8,128)(2,1)S(1)} %all-to-all-done.1.x_ref), custom_call_target="tpu_custom_call" | custom-call | flops 301989888 | bytes 786432 | tf_op jit(solution)/shard_map/pallas_call | solution.py:206
  53.4 3.9 %collective-permute-start.1 = (bf16[768,128]{1,0:T(8,128)(2,1)S(1)}, bf16[768,128]{1,0:T(8,128)(2,1)S(1)}, u32[]{:S(2)}, u32[]{:S(2)}) collective-permute-start(bf16[768,128]{1,0:T(8,128)(2,1)S(1)} %shard_map.49.own_ref), channel_id=1, source_target_pairs={{0,504},{8,0},{16,8},{24,16},{32,24},{40,32},{48,40},{56,48},{64,5... | collective-permute-start | bytes 589832 | tf_op jit(solution)/shard_map/ppermute | solution.py:231
  57.3 1.9 %collective-permute-start = (bf16[768,128]{1,0:T(8,128)(2,1)S(1)}, bf16[768,128]{1,0:T(8,128)(2,1)S(1)}, u32[]{:S(2)}, u32[]{:S(2)}) collective-permute-start(bf16[768,128]{1,0:T(8,128)(2,1)S(1)} %shard_map.49.own_ref), channel_id=1, source_target_pairs={{0,8},{8,16},{16,24},{24,32},{32,40},{40,48},{48,56},{56,64},{64,7... | collective-permute-start | bytes 589832 | tf_op jit(solution)/shard_map/ppermute | solution.py:230
  59.2 3.6 %shard_map.50.toe_ref = bf16[16,2432,128]{2,1,0:T(8,128)(2,1)S(1)} custom-call(bf16[768,128]{1,0:T(8,128)(2,1)S(1)} %shard_map.49.own_ref), custom_call_target="tpu_custom_call" | custom-call | flops 2550136832 | bytes 10158080 | tf_op jit(solution)/shard_map/pallas_call | solution.py:206
  62.8 0.0 collective-permute-done.1.right_ref
  62.8 4.9 %collective-permute-done.left_ref = bf16[768,128]{1,0:T(8,128)(2,1)S(1)} collective-permute-done((bf16[768,128]{1,0:T(8,128)(2,1)S(1)}, bf16[768,128]{1,0:T(8,128)(2,1)S(1)}, u32[]{:S(2)}, u32[]{:S(2)}) %collective-permute-start) | collective-permute-done | bytes 196640 | tf_op jit(solution)/shard_map/ppermute | solution.py:230
  67.7 7.1 %shard_map.51 = f32[9,16,2001]{2,1,0:T(8,128)} custom-call(s32[32]{0:T(128)S(1)} %pad_add_fusion.place_ref, bf16[16,2432,128]{2,1,0:T(8,128)(2,1)S(1)} %shard_map.50.toe_ref, bf16[768,128]{1,0:T(8,128)(2,1)S(1)} %collective-permute-done.left_ref, bf16[768,128]{1,0:T(8,128)(2,1)S(1)} %shard_map.49.own_ref, bf16[768,128]{1,0:T(8,128)(2,1)S(1)} %collective-permute-done.1.right_ref), custom_call_target="tpu_custom_call" | custom-call | flops 1509949440 | bytes 11704000 | tf_op jit(solution)/shard_map/pallas_call | solution.py:206
  (5 shorter events, 0.1 us)
Async XLA Ops:
  0.0 0.8 %copy-start = (bf16[4,8192]{1,0:T(4,128)(2,1)S(1)}, bf16[4,8192]{1,0:T(4,128)(2,1)}, u32[]{:S(2)}) copy-start(bf16[4,8192]{1,0:T(4,128)(2,1)} %x_ref.1) | copy-start | bytes 196612
  1.6 35.9 %all-to-all-start = ((bf16[64,3,4,128]{3,2,1,0:T(4,128)(2,1)}), bf16[64,3,4,128]{3,2,1,0:T(4,128)(2,1)S(1)}, u32[]{:S(2)}, u32[]{:S(2)}) async-start(bf16[64,3,4,128]{3,2,1,0:T(4,128)(2,1)} %shard_map.47), calls=%async_computation | async-start | bytes 393216 | tf_op jit(solution)/shard_map/all_to_all | solution.py:220
  38.6 12.7 %all-to-all-start.1 = ((bf16[8,48,256]{2,1,0:T(8,128)(2,1)}), bf16[8,48,256]{2,1,0:T(8,128)(2,1)S(1)}, u32[]{:S(2)}, u32[]{:S(2)}) async-start(bf16[8,48,256]{2,1,0:T(8,128)(2,1)} %shard_map.48), calls=%async_computation.1 | async-start | bytes 393216 | tf_op jit(solution)/shard_map/all_to_all | solution.py:225
  53.4 9.4 %collective-permute-start.1 = (bf16[768,128]{1,0:T(8,128)(2,1)S(1)}, bf16[768,128]{1,0:T(8,128)(2,1)S(1)}, u32[]{:S(2)}, u32[]{:S(2)}) collective-permute-start(bf16[768,128]{1,0:T(8,128)(2,1)S(1)} %shard_map.49.own_ref), channel_id=1, source_target_pairs={{0,504},{8,0},{16,8},{24,16},{32,24},{40,32},{48,40},{56,48},{64,5... | collective-permute-start | bytes 589832 | tf_op jit(solution)/shard_map/ppermute | solution.py:231
  57.3 10.4 %collective-permute-start = (bf16[768,128]{1,0:T(8,128)(2,1)S(1)}, bf16[768,128]{1,0:T(8,128)(2,1)S(1)}, u32[]{:S(2)}, u32[]{:S(2)}) collective-permute-start(bf16[768,128]{1,0:T(8,128)(2,1)S(1)} %shard_map.49.own_ref), channel_id=1, source_target_pairs={{0,8},{8,16},{16,24},{24,32},{32,40},{40,48},{48,56},{56,64},{64,7... | collective-permute-start | bytes 589832 | tf_op jit(solution)/shard_map/ppermute | solution.py:230

commit v3 on v2

--- a/solution.py
+++ b/solution.py
@@ -80,10 +80,6 @@
 
 def whiten_kernel(filter_ref, x_ref, out_ref):
     lane = lax.broadcasted_iota(jnp.int32, (128, 256), 1)
-    row = lax.broadcasted_iota(jnp.int32, (256, 256), 0)
-    column = lax.broadcasted_iota(jnp.int32, (256, 256), 1)
-    wanted = (2 * (row & 7) + ((row >> 3) & 1)) * 16 + (row >> 4)
-    pick = (column == wanted).astype(jnp.bfloat16)
     for n in range(3):
         here = jnp.concatenate([x_ref[g, 16 * n : 16 * n + 16, :] for g in range(8)], axis=0)
         wide = here.astype(jnp.float32)
@@ -102,9 +98,7 @@
             scale = lax.rsqrt(power[0:1] * (1.0 / SAMPLES) + 1e-06)
             term = banded * scale
             total = term if total is None else total + term
-        turned = lax.dot_general(
-            pick, total.astype(jnp.bfloat16), (((1,), (1,)), ((), ())), preferred_element_type=jnp.float32
-        )
+        turned = jnp.concatenate([total[:, :128].T, total[:, 128:].T], axis=0)
         out_ref[256 * n : 256 * n + 256, :] = turned.astype(jnp.bfloat16)
 
 
@@ -128,7 +122,7 @@
         out_ref[c, 0:128, :] = zero_tile
         for e in range(17):
             if e < 16:
-                wide = jnp.broadcast_to(src[pl.ds(c * 16 + (e % 2) * 8 + e // 2, 1), :], (128, 128))
+                wide = jnp.broadcast_to(src[pl.ds(e * 16 + c, 1), :], (128, 128))
                 rolled = pltpu.roll(wide, 1, 1, stride=1, stride_axis=0)
             else:
                 rolled = jnp.zeros((128, 128), jnp.float32)
@@ -138,38 +132,35 @@
         out_ref[c, 18 * 128 : 19 * 128, :] = zero_tile
         return carry
 
-    lax.fori_loop(0, 16, channel, 0)
-
-
-def correlate_kernel(place_ref, toe_ref, left_ref, own_ref, right_ref, out_ref, rec, lhs_0, lhs_1, res_a, res_b):
-    zeros = jnp.zeros((8, 128), jnp.float32)
-    for i in range(PMAX * 32 + 1):
-        rec[16 * i : 16 * i + 8, :] = zeros
+    lax.fori_loop(0, 16, channel, 0, unroll=4)
+
+
+def correlate_kernel(place_ref, toe_ref, left_ref, own_ref, right_ref, out_ref, rec, lhs_0, lhs_1, res_a, res_b, done, sems):
+    for i in range(PMAX * 2 * 16 * 17 // 8):
+        rec[8 * i : 8 * i + 8, :] = jnp.zeros((8, 128), jnp.float32)
     for k in range(PMAX):
         place = place_ref[k]
         row = pl.multiple_of(place_ref[16 + k], 256)
 
-        @pl.when(place == -1)
-        def _():
-            for i in range(32):
-                rec[(k * 32 + i) * 16 + 8 : (k * 32 + i) * 16 + 16, :] = zeros
-
         for side, ref in enumerate((left_ref, own_ref, right_ref)):
 
             @pl.when(place == side)
             def _():
                 rows = ref[pl.ds(row, 256), :].astype(jnp.float32)
-                for i in range(32):
-                    rec[(k * 32 + i) * 16 + 8 : (k * 32 + i) * 16 + 16, :] = rows[8 * i : 8 * i + 8, :]
+                for b in range(16):
+                    for half in range(2):
+                        first = ((2 * k + b % 2) * 16 + 8 * half) * 17 + 4 + b // 2
+                        at = 16 * b + 8 * half
+                        rec[pl.ds(first, 8, stride=17), :] = rows[at : at + 8, :]
 
     lag_scale = 1.0 / (NB * math.sqrt(SAMPLES))
 
     def fill(lhs, c):
-        first = pl.multiple_of(c * 32, 32)
+        zeros = jnp.zeros((8, 128), jnp.float32)
         for b in range(18):
             parts = []
             for k in range(PMAX):
-                parts.append(rec[pl.ds(first + (k * 512 + (b % 2) * 16 + 4 + b // 2), 8), :])
+                parts.append(rec[pl.ds(c * 17 + ((2 * k + b % 2) * 272 + b // 2), 8), :])
             parts.append(zeros)
             for pair in range(5):
                 both = jnp.concatenate(parts[2 * pair : 2 * pair + 2], axis=0).astype(jnp.bfloat16)
@@ -183,23 +174,34 @@
             res_a[pl.ds(k * 128 + c, 8, stride=16), :] = piece[:, :128]
             res_b[pl.ds(k * 128 + c, 8, stride=16), :] = piece[:, 128:]
 
-    def two(i, carry):
-        fill(lhs_0, 2 * i)
-        fill(lhs_1, 2 * i + 1)
-        work(lhs_0, 2 * i)
-        work(lhs_1, 2 * i + 1)
+    def four(i, carry):
+        fill(lhs_0, 4 * i)
+        fill(lhs_1, 4 * i + 1)
+        work(lhs_0, 4 * i)
+        fill(lhs_0, 4 * i + 2)
+        work(lhs_1, 4 * i + 1)
+        fill(lhs_1, 4 * i + 3)
+        work(lhs_0, 4 * i + 2)
+        work(lhs_1, 4 * i + 3)
         return carry
 
-    lax.fori_loop(0, 8, two, 0)
-    for k in range(PMAX):
-        parts = []
-        for m in range(8):
-            parts.append(res_a[k * 128 + 16 * m : k * 128 + 16 * m + 16, :])
-            parts.append(res_b[k * 128 + 16 * m : k * 128 + 16 * m + 16, :])
-        out_ref[k] = jnp.concatenate(parts, axis=1)[:, SHIFT : SHIFT + LAGS]
-
-
-def call(kernel, out, args, scalars=0, scratch=(), flops=0):
+    copies = []
+    for half in range(2):
+        lax.fori_loop(2 * half, 2 * half + 2, four, 0)
+        for k in range(PMAX):
+            parts = []
+            for m in range(8):
+                at = k * 128 + 16 * m + 8 * half
+                parts.append(res_a[at : at + 8, :])
+                parts.append(res_b[at : at + 8, :])
+            done[half, k] = jnp.concatenate(parts, axis=1)[:, SHIFT : SHIFT + LAGS]
+        copies.append(pltpu.make_async_copy(done.at[half], out_ref.at[:, pl.ds(8 * half, 8), :], sems.at[half]))
+        copies[half].start()
+    for copy in copies:
+        copy.wait()
+
+
+def call(kernel, out, args, scalars=0, scratch=(), flops=0, copied_out=False):
     vmem = pl.BlockSpec(memory_space=pltpu.VMEM)
     smem = pl.BlockSpec(memory_space=pltpu.SMEM)
     size = sum(math.prod(a.shape) * a.dtype.itemsize for a in args) + math.prod(out.shape) * out.dtype.itemsize
@@ -207,7 +209,7 @@
         kernel,
         out_shape=out,
         in_specs=[smem] * scalars + [vmem] * (len(args) - scalars),
-        out_specs=vmem,
+        out_specs=pl.BlockSpec(memory_space=pl.ANY) if copied_out else vmem,
         scratch_shapes=list(scratch),
         compiler_params=pltpu.CompilerParams(vmem_limit_bytes=VMEM_LIMIT),
         cost_estimate=pl.CostEstimate(flops=flops, bytes_accessed=size, transcendentals=0),
@@ -252,12 +254,15 @@
         (places, toe, left, own, right),
         scalars=1,
         scratch=[
-            pltpu.VMEM((PMAX * 512 + 8, 128), jnp.float32),
+            pltpu.VMEM((PMAX * 544, 128), jnp.float32),
             pltpu.VMEM((80, 2304), bf16),
             pltpu.VMEM((80, 2304), bf16),
             pltpu.VMEM((PMAX * 128, 128), jnp.float32),
             pltpu.VMEM((PMAX * 128, 128), jnp.float32),
+            pltpu.VMEM((2, PMAX, 8, LAGS), jnp.float32),
+            pltpu.SemaphoreType.DMA((2,)),
         ],
+        copied_out=True,
         flops=2 * 16 * 80 * 2304 * 256,
     )
 

time: 75.2 us -> 73.3 us (0.975)
  Pallas kernels: 14.9 us -> 12.1 us
  waiting for transfers between devices: 24.7 us -> 25.6 us
    pallas_call x6, Pallas kernels: 14.9 us -> 12.1 us  [call(): pl.pallas_call(kernel, out_shape=out, in_specs=[smem] * scalars + [vmem]...]
    ppermute x1, waiting for transfers between devices: 4.86 us -> 5.75 us  [on_device(): left = lax.ppermute(own, 'tm', [(i, (i + 1) % size) for i in range(size)])]
  transfers between devices with their start and end apart: 4 -> 4, of which waited for: 3 -> 3; matrix products, arithmetic and copies ran while one was open for 2% -> 2% of each run, Pallas kernels for 5% -> 4%
where the time goes in v3:
time: 73.3 us; the launch traced here: 72.9 us
  starting transfers between devices  31.9 us (44%)
  waiting for transfers between devices  25.6 us (35%)
  Pallas kernels  12.1 us (17%)
  other arithmetic  1.68 us (2%)
  local copies, waits for them, and re-layouts  0.84 us (1%)
  between operations  0.74 us (1%)
    all_to_all x1, starting transfers between devices, on_device(): got = lax.all_to_all(sent, 'tm', 0, 0, tiled=True)  19.3 us
    all_to_all x1, waiting for transfers between devices, on_device(): got = lax.all_to_all(sent, 'tm', 0, 0, tiled=True)  15 us
    pallas_call x6, Pallas kernels, call(): pl.pallas_call(kernel, out_shape=out, in_specs=[smem] * scalars + [vmem]...  12.1 us
    all_to_all x1, starting transfers between devices, on_device(): rows = lax.all_to_all(shuffled, 'grp', 0, 0, tiled=True)  6.83 us
    ppermute x1, waiting for transfers between devices, on_device(): left = lax.ppermute(own, 'tm', [(i, (i + 1) % size) for i in range(size)])  5.75 us
    all_to_all x1, waiting for transfers between devices, on_device(): rows = lax.all_to_all(shuffled, 'grp', 0, 0, tiled=True)  4.8 us
    ppermute x1, starting transfers between devices, on_device(): right = lax.ppermute(own, 'tm', [(i, (i - 1) % size) for i in range(size)])  3.91 us
    ppermute x1, starting transfers between devices, on_device(): left = lax.ppermute(own, 'tm', [(i, (i + 1) % size) for i in range(size)])  1.92 us
  transfers between devices with their start and end apart: 4, of which 3 were waited for; matrix products, arithmetic and copies ran while one was open for 2% of the time, Pallas kernels for 4%

profile of v3, /device:TPU:1, one launch (start us, length us, event | category | flops | bytes accessed | tf_op | source)
XLA Modules:
  0.0 72.9 jit_solution(9040246564182754443)
XLA Ops:
  0.0 0.0 copy-start
  0.0 0.8 %copy-done = bf16[4,8192]{1,0:T(4,128)(2,1)S(1)} copy-done((bf16[4,8192]{1,0:T(4,128)(2,1)S(1)}, bf16[4,8192]{1,0:T(4,128)(2,1)}, u32[]{:S(2)}) %copy-start) | copy-done | bytes 65560
  0.8 0.7 shard_map.47
  1.6 19.3 %all-to-all-start = ((bf16[64,3,4,128]{3,2,1,0:T(4,128)(2,1)}), bf16[64,3,4,128]{3,2,1,0:T(4,128)(2,1)S(1)}, u32[]{:S(2)}, u32[]{:S(2)}) async-start(bf16[64,3,4,128]{3,2,1,0:T(4,128)(2,1)} %shard_map.47), calls=%async_computation | async-start | bytes 393216 | tf_op jit(solution)/shard_map/all_to_all | solution.py:222
  21.6 0.7 convert_multiply_fusion
  22.3 0.2 fusion.1.taps_ref
  22.5 15.0 %all-to-all-done.x_ref = bf16[64,3,4,128]{3,2,1,0:T(4,128)(2,1)S(1)} async-done(((bf16[64,3,4,128]{3,2,1,0:T(4,128)(2,1)}), bf16[64,3,4,128]{3,2,1,0:T(4,128)(2,1)S(1)}, u32[]{:S(2)}, u32[]{:S(2)}) %all-to-all-start) | async-done | bytes 196640 | tf_op jit(solution)/shard_map/all_to_all | solution.py:222
  37.5 1.1 %shard_map.48 = bf16[8,48,256]{2,1,0:T(8,128)(2,1)} custom-call(bf16[64,3,4,128]{3,2,1,0:T(4,128)(2,1)S(1)} %all-to-all-done.x_ref), custom_call_target="tpu_custom_call" | custom-call | bytes 393216 | tf_op jit(solution)/shard_map/pallas_call | solution.py:208
  38.6 6.8 %all-to-all-start.1 = ((bf16[8,48,256]{2,1,0:T(8,128)(2,1)}), bf16[8,48,256]{2,1,0:T(8,128)(2,1)S(1)}, u32[]{:S(2)}, u32[]{:S(2)}) async-start(bf16[8,48,256]{2,1,0:T(8,128)(2,1)} %shard_map.48), calls=%async_computation.1 | async-start | bytes 393216 | tf_op jit(solution)/shard_map/all_to_all | solution.py:227
  45.4 0.7 compare_select_fusion
  46.1 0.3 shard_map.46.filter_ref
  46.4 0.1 pad_add_fusion.place_ref
  46.5 4.8 %all-to-all-done.1.x_ref = bf16[8,48,256]{2,1,0:T(8,128)(2,1)S(1)} async-done(((bf16[8,48,256]{2,1,0:T(8,128)(2,1)}), bf16[8,48,256]{2,1,0:T(8,128)(2,1)S(1)}, u32[]{:S(2)}, u32[]{:S(2)}) %all-to-all-start.1) | async-done | bytes 196640 | tf_op jit(solution)/shard_map/all_to_all | solution.py:227
  51.3 1.1 %shard_map.49.own_ref = bf16[768,128]{1,0:T(8,128)(2,1)S(1)} custom-call(bf16[512,384]{1,0:T(8,128)(2,1)S(1)} %shard_map.46.filter_ref, bf16[8,48,256]{2,1,0:T(8,128)(2,1)S(1)} %all-to-all-done.1.x_ref), custom_call_target="tpu_custom_call" | custom-call | flops 301989888 | bytes 786432 | tf_op jit(solution)/shard_map/pallas_call | solution.py:208
  52.4 3.9 %collective-permute-start.1 = (bf16[768,128]{1,0:T(8,128)(2,1)S(1)}, bf16[768,128]{1,0:T(8,128)(2,1)S(1)}, u32[]{:S(2)}, u32[]{:S(2)}) collective-permute-start(bf16[768,128]{1,0:T(8,128)(2,1)S(1)} %shard_map.49.own_ref), channel_id=1, source_target_pairs={{0,504},{8,0},{16,8},{24,16},{32,24},{40,32},{48,40},{56,48},{64,5... | collective-permute-start | bytes 589832 | tf_op jit(solution)/shard_map/ppermute | solution.py:233
  56.3 1.9 %collective-permute-start = (bf16[768,128]{1,0:T(8,128)(2,1)S(1)}, bf16[768,128]{1,0:T(8,128)(2,1)S(1)}, u32[]{:S(2)}, u32[]{:S(2)}) collective-permute-start(bf16[768,128]{1,0:T(8,128)(2,1)S(1)} %shard_map.49.own_ref), channel_id=1, source_target_pairs={{0,8},{8,16},{16,24},{24,32},{32,40},{40,48},{48,56},{56,64},{64,7... | collective-permute-start | bytes 589832 | tf_op jit(solution)/shard_map/ppermute | solution.py:232
  58.2 2.7 %shard_map.50.toe_ref = bf16[16,2432,128]{2,1,0:T(8,128)(2,1)S(1)} custom-call(bf16[768,128]{1,0:T(8,128)(2,1)S(1)} %shard_map.49.own_ref), custom_call_target="tpu_custom_call" | custom-call | flops 2550136832 | bytes 10158080 | tf_op jit(solution)/shard_map/pallas_call | solution.py:208
  60.9 0.0 collective-permute-done.1.right_ref
  60.9 5.8 %collective-permute-done.left_ref = bf16[768,128]{1,0:T(8,128)(2,1)S(1)} collective-permute-done((bf16[768,128]{1,0:T(8,128)(2,1)S(1)}, bf16[768,128]{1,0:T(8,128)(2,1)S(1)}, u32[]{:S(2)}, u32[]{:S(2)}) %collective-permute-start) | collective-permute-done | bytes 196640 | tf_op jit(solution)/shard_map/ppermute | solution.py:232
  66.7 6.3 %shard_map.51 = f32[9,16,2001]{2,1,0:T(8,128)} custom-call(s32[32]{0:T(128)S(1)} %pad_add_fusion.place_ref, bf16[16,2432,128]{2,1,0:T(8,128)(2,1)S(1)} %shard_map.50.toe_ref, bf16[768,128]{1,0:T(8,128)(2,1)S(1)} %collective-permute-done.left_ref, bf16[768,128]{1,0:T(8,128)(2,1)S(1)} %shard_map.49.own_ref, bf16[768,128]{1,0:T(8,128)(2,1)S(1)} %collective-permute-done.1.right_ref), custom_call_target="tpu_custom_call" | custom-call | flops 1509949440 | bytes 11704000 | tf_op jit(solution)/shard_map/pallas_call | solution.py:208
  (5 shorter events, 0.1 us)
Async XLA Ops:
  0.0 0.8 %copy-start = (bf16[4,8192]{1,0:T(4,128)(2,1)S(1)}, bf16[4,8192]{1,0:T(4,128)(2,1)}, u32[]{:S(2)}) copy-start(bf16[4,8192]{1,0:T(4,128)(2,1)} %x_ref.1) | copy-start | bytes 196612
  1.6 35.9 %all-to-all-start = ((bf16[64,3,4,128]{3,2,1,0:T(4,128)(2,1)}), bf16[64,3,4,128]{3,2,1,0:T(4,128)(2,1)S(1)}, u32[]{:S(2)}, u32[]{:S(2)}) async-start(bf16[64,3,4,128]{3,2,1,0:T(4,128)(2,1)} %shard_map.47), calls=%async_computation | async-start | bytes 393216 | tf_op jit(solution)/shard_map/all_to_all | solution.py:222
  38.6 12.7 %all-to-all-start.1 = ((bf16[8,48,256]{2,1,0:T(8,128)(2,1)}), bf16[8,48,256]{2,1,0:T(8,128)(2,1)S(1)}, u32[]{:S(2)}, u32[]{:S(2)}) async-start(bf16[8,48,256]{2,1,0:T(8,128)(2,1)} %shard_map.48), calls=%async_computation.1 | async-start | bytes 393216 | tf_op jit(solution)/shard_map/all_to_all | solution.py:227
  52.4 8.5 %collective-permute-start.1 = (bf16[768,128]{1,0:T(8,128)(2,1)S(1)}, bf16[768,128]{1,0:T(8,128)(2,1)S(1)}, u32[]{:S(2)}, u32[]{:S(2)}) collective-permute-start(bf16[768,128]{1,0:T(8,128)(2,1)S(1)} %shard_map.49.own_ref), channel_id=1, source_target_pairs={{0,504},{8,0},{16,8},{24,16},{32,24},{40,32},{48,40},{56,48},{64,5... | collective-permute-start | bytes 589832 | tf_op jit(solution)/shard_map/ppermute | solution.py:233
  56.3 10.4 %collective-permute-start = (bf16[768,128]{1,0:T(8,128)(2,1)S(1)}, bf16[768,128]{1,0:T(8,128)(2,1)S(1)}, u32[]{:S(2)}, u32[]{:S(2)}) collective-permute-start(bf16[768,128]{1,0:T(8,128)(2,1)S(1)} %shard_map.49.own_ref), channel_id=1, source_target_pairs={{0,8},{8,16},{16,24},{24,32},{32,40},{40,48},{48,56},{56,64},{64,7... | collective-permute-start | bytes 589832 | tf_op jit(solution)/shard_map/ppermute | solution.py:232

commit v4 on v3

--- a/solution.py
+++ b/solution.py
@@ -102,12 +102,17 @@
         out_ref[256 * n : 256 * n + 256, :] = turned.astype(jnp.bfloat16)
 
 
-def spread_kernel(x_ref, out_ref):
-    for o in range(64):
-        block = x_ref[:, 128 * o : 128 * o + 128]
-        out_ref[(o + 3) % 64, 0] = block
-        out_ref[o, 1] = block
-        out_ref[(o - 3) % 64, 2] = block
+def spread_kernel(x_ref, out_ref, sems):
+    parts = ((0, 61, 3, 0), (61, 3, 0, 0), (0, 64, 0, 1), (3, 61, 0, 2), (0, 3, 61, 2))
+    copies = []
+    for i, (start, size, at, n) in enumerate(parts):
+        copies.append(
+            pltpu.make_async_copy(x_ref.at[pl.ds(start, size)], out_ref.at[pl.ds(at, size), n], sems.at[i])
+        )
+    for copy in copies:
+        copy.start()
+    for copy in copies:
+        copy.wait()
 
 
 def toeplitz_kernel(own_ref, out_ref, src):
@@ -195,8 +200,11 @@
                 parts.append(res_a[at : at + 8, :])
                 parts.append(res_b[at : at + 8, :])
             done[half, k] = jnp.concatenate(parts, axis=1)[:, SHIFT : SHIFT + LAGS]
-        copies.append(pltpu.make_async_copy(done.at[half], out_ref.at[:, pl.ds(8 * half, 8), :], sems.at[half]))
-        copies[half].start()
+            copy = pltpu.make_async_copy(
+                done.at[half, k], out_ref.at[k, pl.ds(8 * half, 8), :], sems.at[half, k]
+            )
+            copy.start()
+            copies.append(copy)
     for copy in copies:
         copy.wait()
 
@@ -218,7 +226,14 @@
 
 def on_device(records, band_edges, receiver_block, slot_count):
     bf16 = jnp.bfloat16
-    sent = call(spread_kernel, jax.ShapeDtypeStruct((64, 3, 4, 128), bf16), (records,))
+    sent = pl.pallas_call(
+        spread_kernel,
+        out_shape=jax.ShapeDtypeStruct((64, 3, 4, 128), bf16),
+        in_specs=[pl.BlockSpec(memory_space=pltpu.HBM)],
+        out_specs=pl.BlockSpec(memory_space=pl.ANY),
+        scratch_shapes=[pltpu.SemaphoreType.DMA((5,))],
+        compiler_params=pltpu.CompilerParams(vmem_limit_bytes=62 * 1024 * 1024),
+    )(records.reshape(4, 64, 128).transpose(1, 0, 2))
     got = lax.all_to_all(sent, "tm", 0, 0, tiled=True)
     filters = call(
         filter_kernel, jax.ShapeDtypeStruct((512, 384), bf16), (taps_row(band_edges),), flops=2 * 512 * 384 * 128
@@ -260,7 +275,7 @@
             pltpu.VMEM((PMAX * 128, 128), jnp.float32),
             pltpu.VMEM((PMAX * 128, 128), jnp.float32),
             pltpu.VMEM((2, PMAX, 8, LAGS), jnp.float32),
-            pltpu.SemaphoreType.DMA((2,)),
+            pltpu.SemaphoreType.DMA((2, PMAX)),
         ],
         copied_out=True,
         flops=2 * 16 * 80 * 2304 * 256,

time: 73.3 us -> 78.9 us (1.076)
  Pallas kernels: 12.1 us -> 18.6 us
  local copies, waits for them, and re-layouts: 0.84 us -> 0.01 us
    pallas_call x0 -> x1, Pallas kernels: none -> 7.1 us  [on_device(): pl.pallas_call(spread_kernel, out_shape=jax.ShapeDtypeStruct((64, 3, 4, 1...]
    unnamed x2 -> x0, local copies, waits for them, and re-layouts: 0.84 us -> none
    pallas_call x6 -> x5, Pallas kernels: 12.1 us -> 11.5 us  [call(): pl.pallas_call(kernel, out_shape=out, in_specs=[smem] * scalars + [vmem]...]
where the time goes in v4:
time: 78.9 us; the launch traced here: 78.5 us
  starting transfers between devices  31.9 us (40%)
  waiting for transfers between devices  25.6 us (32%)
  Pallas kernels  18.6 us (24%)
  other arithmetic  1.68 us (2%)
    all_to_all x1, starting transfers between devices, on_device(): got = lax.all_to_all(sent, 'tm', 0, 0, tiled=True)  19.3 us
    all_to_all x1, waiting for transfers between devices, on_device(): got = lax.all_to_all(sent, 'tm', 0, 0, tiled=True)  15 us
    pallas_call x5, Pallas kernels, call(): pl.pallas_call(kernel, out_shape=out, in_specs=[smem] * scalars + [vmem]...  11.5 us
    pallas_call x1, Pallas kernels, on_device(): pl.pallas_call(spread_kernel, out_shape=jax.ShapeDtypeStruct((64, 3, 4, 1...  7.1 us
    all_to_all x1, starting transfers between devices, on_device(): rows = lax.all_to_all(shuffled, 'grp', 0, 0, tiled=True)  6.83 us
    ppermute x1, waiting for transfers between devices, on_device(): left = lax.ppermute(own, 'tm', [(i, (i + 1) % size) for i in range(size)])  5.75 us
    all_to_all x1, waiting for transfers between devices, on_device(): rows = lax.all_to_all(shuffled, 'grp', 0, 0, tiled=True)  4.8 us
    ppermute x1, starting transfers between devices, on_device(): right = lax.ppermute(own, 'tm', [(i, (i - 1) % size) for i in range(size)])  3.91 us
  transfers between devices with their start and end apart: 4, of which 3 were waited for; matrix products, arithmetic and copies ran while one was open for 2% of the time, Pallas kernels for 4%

profile of v4, /device:TPU:1, one launch (start us, length us, event | category | flops | bytes accessed | tf_op | source)
XLA Modules:
  0.0 78.5 jit_solution(1857512606608143239)
XLA Ops:
  0.0 7.1 %shard_map.47 = bf16[64,3,4,128]{3,2,1,0:T(4,128)(2,1)} custom-call(bf16[64,4,128]{2,1,0:T(4,128)(2,1)} %bitcast.26), custom_call_target="tpu_custom_call" | custom-call | tf_op jit(solution)/shard_map/pallas_call | solution.py:229
  7.1 19.3 %all-to-all-start = ((bf16[64,3,4,128]{3,2,1,0:T(4,128)(2,1)}), bf16[64,3,4,128]{3,2,1,0:T(4,128)(2,1)S(1)}, u32[]{:S(2)}, u32[]{:S(2)}) async-start(bf16[64,3,4,128]{3,2,1,0:T(4,128)(2,1)} %shard_map.47), calls=%async_computation | async-start | bytes 393216 | tf_op jit(solution)/shard_map/all_to_all | solution.py:237
  27.1 0.7 convert_multiply_fusion
  27.8 0.2 fusion.1.taps_ref
  28.0 15.0 %all-to-all-done.x_ref = bf16[64,3,4,128]{3,2,1,0:T(4,128)(2,1)S(1)} async-done(((bf16[64,3,4,128]{3,2,1,0:T(4,128)(2,1)}), bf16[64,3,4,128]{3,2,1,0:T(4,128)(2,1)S(1)}, u32[]{:S(2)}, u32[]{:S(2)}) %all-to-all-start) | async-done | bytes 196640 | tf_op jit(solution)/shard_map/all_to_all | solution.py:237
  43.0 1.1 %shard_map.48 = bf16[8,48,256]{2,1,0:T(8,128)(2,1)} custom-call(bf16[64,3,4,128]{3,2,1,0:T(4,128)(2,1)S(1)} %all-to-all-done.x_ref), custom_call_target="tpu_custom_call" | custom-call | bytes 393216 | tf_op jit(solution)/shard_map/pallas_call | solution.py:216
  44.2 6.8 %all-to-all-start.1 = ((bf16[8,48,256]{2,1,0:T(8,128)(2,1)}), bf16[8,48,256]{2,1,0:T(8,128)(2,1)S(1)}, u32[]{:S(2)}, u32[]{:S(2)}) async-start(bf16[8,48,256]{2,1,0:T(8,128)(2,1)} %shard_map.48), calls=%async_computation.1 | async-start | bytes 393216 | tf_op jit(solution)/shard_map/all_to_all | solution.py:242
  51.0 0.7 compare_select_fusion
  51.7 0.3 shard_map.46.filter_ref
  52.0 0.1 pad_add_fusion.place_ref
  52.1 4.8 %all-to-all-done.1.x_ref = bf16[8,48,256]{2,1,0:T(8,128)(2,1)S(1)} async-done(((bf16[8,48,256]{2,1,0:T(8,128)(2,1)}), bf16[8,48,256]{2,1,0:T(8,128)(2,1)S(1)}, u32[]{:S(2)}, u32[]{:S(2)}) %all-to-all-start.1) | async-done | bytes 196640 | tf_op jit(solution)/shard_map/all_to_all | solution.py:242
  56.9 1.1 %shard_map.49.own_ref = bf16[768,128]{1,0:T(8,128)(2,1)S(1)} custom-call(bf16[512,384]{1,0:T(8,128)(2,1)S(1)} %shard_map.46.filter_ref, bf16[8,48,256]{2,1,0:T(8,128)(2,1)S(1)} %all-to-all-done.1.x_ref), custom_call_target="tpu_custom_call" | custom-call | flops 301989888 | bytes 786432 | tf_op jit(solution)/shard_map/pallas_call | solution.py:216
  57.9 3.9 %collective-permute-start.1 = (bf16[768,128]{1,0:T(8,128)(2,1)S(1)}, bf16[768,128]{1,0:T(8,128)(2,1)S(1)}, u32[]{:S(2)}, u32[]{:S(2)}) collective-permute-start(bf16[768,128]{1,0:T(8,128)(2,1)S(1)} %shard_map.49.own_ref), channel_id=1, source_target_pairs={{0,504},{8,0},{16,8},{24,16},{32,24},{40,32},{48,40},{56,48},{64,5... | collective-permute-start | bytes 589832 | tf_op jit(solution)/shard_map/ppermute | solution.py:248
  61.9 1.9 %collective-permute-start = (bf16[768,128]{1,0:T(8,128)(2,1)S(1)}, bf16[768,128]{1,0:T(8,128)(2,1)S(1)}, u32[]{:S(2)}, u32[]{:S(2)}) collective-permute-start(bf16[768,128]{1,0:T(8,128)(2,1)S(1)} %shard_map.49.own_ref), channel_id=1, source_target_pairs={{0,8},{8,16},{16,24},{24,32},{32,40},{40,48},{48,56},{56,64},{64,7... | collective-permute-start | bytes 589832 | tf_op jit(solution)/shard_map/ppermute | solution.py:247
  63.8 2.7 %shard_map.50.toe_ref = bf16[16,2432,128]{2,1,0:T(8,128)(2,1)S(1)} custom-call(bf16[768,128]{1,0:T(8,128)(2,1)S(1)} %shard_map.49.own_ref), custom_call_target="tpu_custom_call" | custom-call | flops 2550136832 | bytes 10158080 | tf_op jit(solution)/shard_map/pallas_call | solution.py:216
  66.5 0.0 collective-permute-done.1.right_ref
  66.5 5.8 %collective-permute-done.left_ref = bf16[768,128]{1,0:T(8,128)(2,1)S(1)} collective-permute-done((bf16[768,128]{1,0:T(8,128)(2,1)S(1)}, bf16[768,128]{1,0:T(8,128)(2,1)S(1)}, u32[]{:S(2)}, u32[]{:S(2)}) %collective-permute-start) | collective-permute-done | bytes 196640 | tf_op jit(solution)/shard_map/ppermute | solution.py:247
  72.2 6.3 %shard_map.51 = f32[9,16,2001]{2,1,0:T(8,128)} custom-call(s32[32]{0:T(128)S(1)} %pad_add_fusion.place_ref, bf16[16,2432,128]{2,1,0:T(8,128)(2,1)S(1)} %shard_map.50.toe_ref, bf16[768,128]{1,0:T(8,128)(2,1)S(1)} %collective-permute-done.left_ref, bf16[768,128]{1,0:T(8,128)(2,1)S(1)} %shard_map.49.own_ref, bf16[768,128]{1,0:T(8,128)(2,1)S(1)} %collective-permute-done.1.right_ref), custom_call_target="tpu_custom_call" | custom-call | flops 1509949440 | bytes 11704000 | tf_op jit(solution)/shard_map/pallas_call | solution.py:216
  (5 shorter events, 0.1 us)
Async XLA Ops:
  7.1 35.9 %all-to-all-start = ((bf16[64,3,4,128]{3,2,1,0:T(4,128)(2,1)}), bf16[64,3,4,128]{3,2,1,0:T(4,128)(2,1)S(1)}, u32[]{:S(2)}, u32[]{:S(2)}) async-start(bf16[64,3,4,128]{3,2,1,0:T(4,128)(2,1)} %shard_map.47), calls=%async_computation | async-start | bytes 393216 | tf_op jit(solution)/shard_map/all_to_all | solution.py:237
  44.2 12.7 %all-to-all-start.1 = ((bf16[8,48,256]{2,1,0:T(8,128)(2,1)}), bf16[8,48,256]{2,1,0:T(8,128)(2,1)S(1)}, u32[]{:S(2)}, u32[]{:S(2)}) async-start(bf16[8,48,256]{2,1,0:T(8,128)(2,1)} %shard_map.48), calls=%async_computation.1 | async-start | bytes 393216 | tf_op jit(solution)/shard_map/all_to_all | solution.py:242
  57.9 8.5 %collective-permute-start.1 = (bf16[768,128]{1,0:T(8,128)(2,1)S(1)}, bf16[768,128]{1,0:T(8,128)(2,1)S(1)}, u32[]{:S(2)}, u32[]{:S(2)}) collective-permute-start(bf16[768,128]{1,0:T(8,128)(2,1)S(1)} %shard_map.49.own_ref), channel_id=1, source_target_pairs={{0,504},{8,0},{16,8},{24,16},{32,24},{40,32},{48,40},{56,48},{64,5... | collective-permute-start | bytes 589832 | tf_op jit(solution)/shard_map/ppermute | solution.py:248
  61.9 10.4 %collective-permute-start = (bf16[768,128]{1,0:T(8,128)(2,1)S(1)}, bf16[768,128]{1,0:T(8,128)(2,1)S(1)}, u32[]{:S(2)}, u32[]{:S(2)}) collective-permute-start(bf16[768,128]{1,0:T(8,128)(2,1)S(1)} %shard_map.49.own_ref), channel_id=1, source_target_pairs={{0,8},{8,16},{16,24},{24,32},{32,40},{40,48},{48,56},{56,64},{64,7... | collective-permute-start | bytes 589832 | tf_op jit(solution)/shard_map/ppermute | solution.py:247

commit v5 on v3

--- a/solution.py
+++ b/solution.py
@@ -69,13 +69,16 @@
             for b in range(8 * tile, 8 * tile + 8):
                 parts = [x_ref[4 * b + q, n].astype(jnp.float32) for q in range(4)]
                 rows.append(jnp.concatenate(parts, axis=0))
+            for step in (4, 2, 1):
+                upper = (group & step) != 0
+                for i in range(8):
+                    if i & step:
+                        continue
+                    low, high = rows[i], rows[i + step]
+                    rows[i] = jnp.where(upper, pltpu.roll(high, 16 * step, 1), low)
+                    rows[i + step] = jnp.where(upper, high, pltpu.roll(low, 128 - 16 * step, 1))
             for g in range(8):
-                total = None
-                for l in range(8):
-                    turn = (16 * (l - g)) % 128
-                    moved = rows[l] if turn == 0 else pltpu.roll(rows[l], turn, 1)
-                    total = moved if total is None else jnp.where(group == l, moved, total)
-                out_ref[g, 16 * n : 16 * n + 16, 128 * tile : 128 * tile + 128] = total.astype(jnp.bfloat16)
+                out_ref[g, 16 * n : 16 * n + 16, 128 * tile : 128 * tile + 128] = rows[g].astype(jnp.bfloat16)
 
 
 def whiten_kernel(filter_ref, x_ref, out_ref):
@@ -135,7 +138,7 @@
     lax.fori_loop(0, 16, channel, 0, unroll=4)
 
 
-def correlate_kernel(place_ref, toe_ref, left_ref, own_ref, right_ref, out_ref, rec, lhs_0, lhs_1, res_a, res_b, done, sems):
+def correlate_kernel(place_ref, toe_ref, left_ref, own_ref, right_ref, out_ref, rec, lhs, res_a, res_b, done, sems):
     for i in range(PMAX * 2 * 16 * 17 // 8):
         rec[8 * i : 8 * i + 8, :] = jnp.zeros((8, 128), jnp.float32)
     for k in range(PMAX):
@@ -174,20 +177,13 @@
             res_a[pl.ds(k * 128 + c, 8, stride=16), :] = piece[:, :128]
             res_b[pl.ds(k * 128 + c, 8, stride=16), :] = piece[:, 128:]
 
-    def four(i, carry):
-        fill(lhs_0, 4 * i)
-        fill(lhs_1, 4 * i + 1)
-        work(lhs_0, 4 * i)
-        fill(lhs_0, 4 * i + 2)
-        work(lhs_1, 4 * i + 1)
-        fill(lhs_1, 4 * i + 3)
-        work(lhs_0, 4 * i + 2)
-        work(lhs_1, 4 * i + 3)
-        return carry
-
     copies = []
     for half in range(2):
-        lax.fori_loop(2 * half, 2 * half + 2, four, 0)
+        for c in range(8 * half, 8 * half + 8):
+            fill(lhs.at[c % 4], c)
+            if c % 8 >= 1:
+                work(lhs.at[(c - 1) % 4], c - 1)
+        work(lhs.at[3], 8 * half + 7)
         for k in range(PMAX):
             parts = []
             for m in range(8):
@@ -195,8 +191,11 @@
                 parts.append(res_a[at : at + 8, :])
                 parts.append(res_b[at : at + 8, :])
             done[half, k] = jnp.concatenate(parts, axis=1)[:, SHIFT : SHIFT + LAGS]
-        copies.append(pltpu.make_async_copy(done.at[half], out_ref.at[:, pl.ds(8 * half, 8), :], sems.at[half]))
-        copies[half].start()
+            copy = pltpu.make_async_copy(
+                done.at[half, k], out_ref.at[k, pl.ds(8 * half, 8), :], sems.at[half, k]
+            )
+            copy.start()
+            copies.append(copy)
     for copy in copies:
         copy.wait()
 
@@ -255,12 +254,11 @@
         scalars=1,
         scratch=[
             pltpu.VMEM((PMAX * 544, 128), jnp.float32),
-            pltpu.VMEM((80, 2304), bf16),
-            pltpu.VMEM((80, 2304), bf16),
+            pltpu.VMEM((4, 80, 2304), bf16),
             pltpu.VMEM((PMAX * 128, 128), jnp.float32),
             pltpu.VMEM((PMAX * 128, 128), jnp.float32),
             pltpu.VMEM((2, PMAX, 8, LAGS), jnp.float32),
-            pltpu.SemaphoreType.DMA((2,)),
+            pltpu.SemaphoreType.DMA((2, PMAX)),
         ],
         copied_out=True,
         flops=2 * 16 * 80 * 2304 * 256,

time: 73.3 us -> 72.7 us (level)
  no operation moved by 1% of the time
where the time goes in v5:
time: 72.7 us; the launch traced here: 72.3 us
  starting transfers between devices  31.9 us (44%)
  waiting for transfers between devices  25.6 us (35%)
  Pallas kernels  11.5 us (16%)
  other arithmetic  1.68 us (2%)
  local copies, waits for them, and re-layouts  0.84 us (1%)
  between operations  0.74 us (1%)
    all_to_all x1, starting transfers between devices, on_device(): got = lax.all_to_all(sent, 'tm', 0, 0, tiled=True)  19.3 us
    all_to_all x1, waiting for transfers between devices, on_device(): got = lax.all_to_all(sent, 'tm', 0, 0, tiled=True)  15 us
    pallas_call x6, Pallas kernels, call(): pl.pallas_call(kernel, out_shape=out, in_specs=[smem] * scalars + [vmem]...  11.5 us
    all_to_all x1, starting transfers between devices, on_device(): rows = lax.all_to_all(shuffled, 'grp', 0, 0, tiled=True)  6.83 us
    ppermute x1, waiting for transfers between devices, on_device(): left = lax.ppermute(own, 'tm', [(i, (i + 1) % size) for i in range(size)])  5.76 us
    all_to_all x1, waiting for transfers between devices, on_device(): rows = lax.all_to_all(shuffled, 'grp', 0, 0, tiled=True)  4.8 us
    ppermute x1, starting transfers between devices, on_device(): right = lax.ppermute(own, 'tm', [(i, (i - 1) % size) for i in range(size)])  3.91 us
    ppermute x1, starting transfers between devices, on_device(): left = lax.ppermute(own, 'tm', [(i, (i + 1) % size) for i in range(size)])  1.92 us
  transfers between devices with their start and end apart: 4, of which 3 were waited for; matrix products, arithmetic and copies ran while one was open for 2% of the time, Pallas kernels for 4%

profile of v5, /device:TPU:1, one launch (start us, length us, event | category | flops | bytes accessed | tf_op | source)
XLA Modules:
  0.0 72.3 jit_solution(14033692524101333213)
XLA Ops:
  0.0 0.0 copy-start
  0.0 0.8 %copy-done = bf16[4,8192]{1,0:T(4,128)(2,1)S(1)} copy-done((bf16[4,8192]{1,0:T(4,128)(2,1)S(1)}, bf16[4,8192]{1,0:T(4,128)(2,1)}, u32[]{:S(2)}) %copy-start) | copy-done | bytes 65560
  0.8 0.7 %shard_map.47 = bf16[64,3,4,128]{3,2,1,0:T(4,128)(2,1)} custom-call(bf16[4,8192]{1,0:T(4,128)(2,1)S(1)} %copy-done), custom_call_target="tpu_custom_call" | custom-call | bytes 262144 | tf_op jit(solution)/shard_map/pallas_call | solution.py:207
  1.6 19.3 %all-to-all-start = ((bf16[64,3,4,128]{3,2,1,0:T(4,128)(2,1)}), bf16[64,3,4,128]{3,2,1,0:T(4,128)(2,1)S(1)}, u32[]{:S(2)}, u32[]{:S(2)}) async-start(bf16[64,3,4,128]{3,2,1,0:T(4,128)(2,1)} %shard_map.47), calls=%async_computation | async-start | bytes 393216 | tf_op jit(solution)/shard_map/all_to_all | solution.py:221
  21.6 0.7 convert_multiply_fusion
  22.3 0.2 fusion.1.taps_ref
  22.5 15.0 %all-to-all-done.x_ref = bf16[64,3,4,128]{3,2,1,0:T(4,128)(2,1)S(1)} async-done(((bf16[64,3,4,128]{3,2,1,0:T(4,128)(2,1)}), bf16[64,3,4,128]{3,2,1,0:T(4,128)(2,1)S(1)}, u32[]{:S(2)}, u32[]{:S(2)}) %all-to-all-start) | async-done | bytes 196640 | tf_op jit(solution)/shard_map/all_to_all | solution.py:221
  37.5 1.0 %shard_map.48 = bf16[8,48,256]{2,1,0:T(8,128)(2,1)} custom-call(bf16[64,3,4,128]{3,2,1,0:T(4,128)(2,1)S(1)} %all-to-all-done.x_ref), custom_call_target="tpu_custom_call" | custom-call | bytes 393216 | tf_op jit(solution)/shard_map/pallas_call | solution.py:207
  38.5 6.8 %all-to-all-start.1 = ((bf16[8,48,256]{2,1,0:T(8,128)(2,1)}), bf16[8,48,256]{2,1,0:T(8,128)(2,1)S(1)}, u32[]{:S(2)}, u32[]{:S(2)}) async-start(bf16[8,48,256]{2,1,0:T(8,128)(2,1)} %shard_map.48), calls=%async_computation.1 | async-start | bytes 393216 | tf_op jit(solution)/shard_map/all_to_all | solution.py:226
  45.3 0.7 compare_select_fusion
  46.0 0.3 shard_map.46.filter_ref
  46.4 0.1 pad_add_fusion.place_ref
  46.4 4.8 %all-to-all-done.1.x_ref = bf16[8,48,256]{2,1,0:T(8,128)(2,1)S(1)} async-done(((bf16[8,48,256]{2,1,0:T(8,128)(2,1)}), bf16[8,48,256]{2,1,0:T(8,128)(2,1)S(1)}, u32[]{:S(2)}, u32[]{:S(2)}) %all-to-all-start.1) | async-done | bytes 196640 | tf_op jit(solution)/shard_map/all_to_all | solution.py:226
  51.2 1.1 %shard_map.49.own_ref = bf16[768,128]{1,0:T(8,128)(2,1)S(1)} custom-call(bf16[512,384]{1,0:T(8,128)(2,1)S(1)} %shard_map.46.filter_ref, bf16[8,48,256]{2,1,0:T(8,128)(2,1)S(1)} %all-to-all-done.1.x_ref), custom_call_target="tpu_custom_call" | custom-call | flops 301989888 | bytes 786432 | tf_op jit(solution)/shard_map/pallas_call | solution.py:207
  52.3 3.9 %collective-permute-start.1 = (bf16[768,128]{1,0:T(8,128)(2,1)S(1)}, bf16[768,128]{1,0:T(8,128)(2,1)S(1)}, u32[]{:S(2)}, u32[]{:S(2)}) collective-permute-start(bf16[768,128]{1,0:T(8,128)(2,1)S(1)} %shard_map.49.own_ref), channel_id=1, source_target_pairs={{0,504},{8,0},{16,8},{24,16},{32,24},{40,32},{48,40},{56,48},{64,5... | collective-permute-start | bytes 589832 | tf_op jit(solution)/shard_map/ppermute | solution.py:232
  56.2 1.9 %collective-permute-start = (bf16[768,128]{1,0:T(8,128)(2,1)S(1)}, bf16[768,128]{1,0:T(8,128)(2,1)S(1)}, u32[]{:S(2)}, u32[]{:S(2)}) collective-permute-start(bf16[768,128]{1,0:T(8,128)(2,1)S(1)} %shard_map.49.own_ref), channel_id=1, source_target_pairs={{0,8},{8,16},{16,24},{24,32},{32,40},{40,48},{48,56},{56,64},{64,7... | collective-permute-start | bytes 589832 | tf_op jit(solution)/shard_map/ppermute | solution.py:231
  58.1 2.7 %shard_map.50.toe_ref = bf16[16,2432,128]{2,1,0:T(8,128)(2,1)S(1)} custom-call(bf16[768,128]{1,0:T(8,128)(2,1)S(1)} %shard_map.49.own_ref), custom_call_target="tpu_custom_call" | custom-call | flops 2550136832 | bytes 10158080 | tf_op jit(solution)/shard_map/pallas_call | solution.py:207
  60.8 0.0 collective-permute-done.1.right_ref
  60.8 5.8 %collective-permute-done.left_ref = bf16[768,128]{1,0:T(8,128)(2,1)S(1)} collective-permute-done((bf16[768,128]{1,0:T(8,128)(2,1)S(1)}, bf16[768,128]{1,0:T(8,128)(2,1)S(1)}, u32[]{:S(2)}, u32[]{:S(2)}) %collective-permute-start) | collective-permute-done | bytes 196640 | tf_op jit(solution)/shard_map/ppermute | solution.py:231
  66.6 5.7 %shard_map.51 = f32[9,16,2001]{2,1,0:T(8,128)} custom-call(s32[32]{0:T(128)S(1)} %pad_add_fusion.place_ref, bf16[16,2432,128]{2,1,0:T(8,128)(2,1)S(1)} %shard_map.50.toe_ref, bf16[768,128]{1,0:T(8,128)(2,1)S(1)} %collective-permute-done.left_ref, bf16[768,128]{1,0:T(8,128)(2,1)S(1)} %shard_map.49.own_ref, bf16[768,128]{1,0:T(8,128)(2,1)S(1)} %collective-permute-done.1.right_ref), custom_call_target="tpu_custom_call" | custom-call | flops 1509949440 | bytes 11704000 | tf_op jit(solution)/shard_map/pallas_call | solution.py:207
  (5 shorter events, 0.1 us)
Async XLA Ops:
  0.0 0.8 %copy-start = (bf16[4,8192]{1,0:T(4,128)(2,1)S(1)}, bf16[4,8192]{1,0:T(4,128)(2,1)}, u32[]{:S(2)}) copy-start(bf16[4,8192]{1,0:T(4,128)(2,1)} %x_ref.1) | copy-start | bytes 196612
  1.6 35.9 %all-to-all-start = ((bf16[64,3,4,128]{3,2,1,0:T(4,128)(2,1)}), bf16[64,3,4,128]{3,2,1,0:T(4,128)(2,1)S(1)}, u32[]{:S(2)}, u32[]{:S(2)}) async-start(bf16[64,3,4,128]{3,2,1,0:T(4,128)(2,1)} %shard_map.47), calls=%async_computation | async-start | bytes 393216 | tf_op jit(solution)/shard_map/all_to_all | solution.py:221
  38.5 12.7 %all-to-all-start.1 = ((bf16[8,48,256]{2,1,0:T(8,128)(2,1)}), bf16[8,48,256]{2,1,0:T(8,128)(2,1)S(1)}, u32[]{:S(2)}, u32[]{:S(2)}) async-start(bf16[8,48,256]{2,1,0:T(8,128)(2,1)} %shard_map.48), calls=%async_computation.1 | async-start | bytes 393216 | tf_op jit(solution)/shard_map/all_to_all | solution.py:226
  52.3 8.5 %collective-permute-start.1 = (bf16[768,128]{1,0:T(8,128)(2,1)S(1)}, bf16[768,128]{1,0:T(8,128)(2,1)S(1)}, u32[]{:S(2)}, u32[]{:S(2)}) collective-permute-start(bf16[768,128]{1,0:T(8,128)(2,1)S(1)} %shard_map.49.own_ref), channel_id=1, source_target_pairs={{0,504},{8,0},{16,8},{24,16},{32,24},{40,32},{48,40},{56,48},{64,5... | collective-permute-start | bytes 589832 | tf_op jit(solution)/shard_map/ppermute | solution.py:232
  56.2 10.4 %collective-permute-start = (bf16[768,128]{1,0:T(8,128)(2,1)S(1)}, bf16[768,128]{1,0:T(8,128)(2,1)S(1)}, u32[]{:S(2)}, u32[]{:S(2)}) collective-permute-start(bf16[768,128]{1,0:T(8,128)(2,1)S(1)} %shard_map.49.own_ref), channel_id=1, source_target_pairs={{0,8},{8,16},{16,24},{24,32},{32,40},{40,48},{48,56},{56,64},{64,7... | collective-permute-start | bytes 589832 | tf_op jit(solution)/shard_map/ppermute | solution.py:231

commit v6 on v5

--- a/solution.py
+++ b/solution.py
@@ -228,8 +228,8 @@
         whiten_kernel, jax.ShapeDtypeStruct((768, 128), bf16), (filters, rows), flops=2 * 3 * 512 * 384 * 256
     )
     size = lax.axis_size("tm")
+    right = lax.ppermute(own, "tm", [(i, (i - 1) % size) for i in range(size)])
     left = lax.ppermute(own, "tm", [(i, (i + 1) % size) for i in range(size)])
-    right = lax.ppermute(own, "tm", [(i, (i - 1) % size) for i in range(size)])
     toe = call(
         toeplitz_kernel,
         jax.ShapeDtypeStruct((16, 2432, 128), bf16),

time: 72.7 us -> 72.7 us (level)
  no operation moved by 1% of the time
where the time goes in v6:
time: 72.7 us; the launch traced here: 72.3 us
  starting transfers between devices  31.9 us (44%)
  waiting for transfers between devices  25.6 us (35%)
  Pallas kernels  11.5 us (16%)
  other arithmetic  1.68 us (2%)
  local copies, waits for them, and re-layouts  0.84 us (1%)
  between operations  0.74 us (1%)
    all_to_all x1, starting transfers between devices, on_device(): got = lax.all_to_all(sent, 'tm', 0, 0, tiled=True)  19.3 us
    all_to_all x1, waiting for transfers between devices, on_device(): got = lax.all_to_all(sent, 'tm', 0, 0, tiled=True)  15 us
    pallas_call x6, Pallas kernels, call(): pl.pallas_call(kernel, out_shape=out, in_specs=[smem] * scalars + [vmem]...  11.5 us
    all_to_all x1, starting transfers between devices, on_device(): rows = lax.all_to_all(shuffled, 'grp', 0, 0, tiled=True)  6.83 us
    ppermute x1, waiting for transfers between devices, on_device(): left = lax.ppermute(own, 'tm', [(i, (i + 1) % size) for i in range(size)])  5.76 us
    all_to_all x1, waiting for transfers between devices, on_device(): rows = lax.all_to_all(shuffled, 'grp', 0, 0, tiled=True)  4.8 us
    ppermute x1, starting transfers between devices, on_device(): right = lax.ppermute(own, 'tm', [(i, (i - 1) % size) for i in range(size)])  3.91 us
    ppermute x1, starting transfers between devices, on_device(): left = lax.ppermute(own, 'tm', [(i, (i + 1) % size) for i in range(size)])  1.92 us
  transfers between devices with their start and end apart: 4, of which 3 were waited for; matrix products, arithmetic and copies ran while one was open for 2% of the time, Pallas kernels for 4%

profile of v6, /device:TPU:1, one launch (start us, length us, event | category | flops | bytes accessed | tf_op | source)
XLA Modules:
  0.0 72.3 jit_solution(14033692524101333213)
XLA Ops:
  0.0 0.0 copy-start
  0.0 0.8 %copy-done = bf16[4,8192]{1,0:T(4,128)(2,1)S(1)} copy-done((bf16[4,8192]{1,0:T(4,128)(2,1)S(1)}, bf16[4,8192]{1,0:T(4,128)(2,1)}, u32[]{:S(2)}) %copy-start) | copy-done | bytes 65560
  0.8 0.7 %shard_map.47 = bf16[64,3,4,128]{3,2,1,0:T(4,128)(2,1)} custom-call(bf16[4,8192]{1,0:T(4,128)(2,1)S(1)} %copy-done), custom_call_target="tpu_custom_call" | custom-call | bytes 262144 | tf_op jit(solution)/shard_map/pallas_call | solution.py:207
  1.6 19.3 %all-to-all-start = ((bf16[64,3,4,128]{3,2,1,0:T(4,128)(2,1)}), bf16[64,3,4,128]{3,2,1,0:T(4,128)(2,1)S(1)}, u32[]{:S(2)}, u32[]{:S(2)}) async-start(bf16[64,3,4,128]{3,2,1,0:T(4,128)(2,1)} %shard_map.47), calls=%async_computation | async-start | bytes 393216 | tf_op jit(solution)/shard_map/all_to_all | solution.py:221
  21.6 0.7 convert_multiply_fusion
  22.3 0.2 fusion.1.taps_ref
  22.5 15.0 %all-to-all-done.x_ref = bf16[64,3,4,128]{3,2,1,0:T(4,128)(2,1)S(1)} async-done(((bf16[64,3,4,128]{3,2,1,0:T(4,128)(2,1)}), bf16[64,3,4,128]{3,2,1,0:T(4,128)(2,1)S(1)}, u32[]{:S(2)}, u32[]{:S(2)}) %all-to-all-start) | async-done | bytes 196640 | tf_op jit(solution)/shard_map/all_to_all | solution.py:221
  37.5 1.0 %shard_map.48 = bf16[8,48,256]{2,1,0:T(8,128)(2,1)} custom-call(bf16[64,3,4,128]{3,2,1,0:T(4,128)(2,1)S(1)} %all-to-all-done.x_ref), custom_call_target="tpu_custom_call" | custom-call | bytes 393216 | tf_op jit(solution)/shard_map/pallas_call | solution.py:207
  38.5 6.8 %all-to-all-start.1 = ((bf16[8,48,256]{2,1,0:T(8,128)(2,1)}), bf16[8,48,256]{2,1,0:T(8,128)(2,1)S(1)}, u32[]{:S(2)}, u32[]{:S(2)}) async-start(bf16[8,48,256]{2,1,0:T(8,128)(2,1)} %shard_map.48), calls=%async_computation.1 | async-start | bytes 393216 | tf_op jit(solution)/shard_map/all_to_all | solution.py:226
  45.3 0.7 compare_select_fusion
  46.0 0.3 shard_map.46.filter_ref
  46.4 0.1 pad_add_fusion.place_ref
  46.4 4.8 %all-to-all-done.1.x_ref = bf16[8,48,256]{2,1,0:T(8,128)(2,1)S(1)} async-done(((bf16[8,48,256]{2,1,0:T(8,128)(2,1)}), bf16[8,48,256]{2,1,0:T(8,128)(2,1)S(1)}, u32[]{:S(2)}, u32[]{:S(2)}) %all-to-all-start.1) | async-done | bytes 196640 | tf_op jit(solution)/shard_map/all_to_all | solution.py:226
  51.2 1.1 %shard_map.49.own_ref = bf16[768,128]{1,0:T(8,128)(2,1)S(1)} custom-call(bf16[512,384]{1,0:T(8,128)(2,1)S(1)} %shard_map.46.filter_ref, bf16[8,48,256]{2,1,0:T(8,128)(2,1)S(1)} %all-to-all-done.1.x_ref), custom_call_target="tpu_custom_call" | custom-call | flops 301989888 | bytes 786432 | tf_op jit(solution)/shard_map/pallas_call | solution.py:207
  52.3 3.9 %collective-permute-start.1 = (bf16[768,128]{1,0:T(8,128)(2,1)S(1)}, bf16[768,128]{1,0:T(8,128)(2,1)S(1)}, u32[]{:S(2)}, u32[]{:S(2)}) collective-permute-start(bf16[768,128]{1,0:T(8,128)(2,1)S(1)} %shard_map.49.own_ref), channel_id=1, source_target_pairs={{0,504},{8,0},{16,8},{24,16},{32,24},{40,32},{48,40},{56,48},{64,5... | collective-permute-start | bytes 589832 | tf_op jit(solution)/shard_map/ppermute | solution.py:231
  56.2 1.9 %collective-permute-start = (bf16[768,128]{1,0:T(8,128)(2,1)S(1)}, bf16[768,128]{1,0:T(8,128)(2,1)S(1)}, u32[]{:S(2)}, u32[]{:S(2)}) collective-permute-start(bf16[768,128]{1,0:T(8,128)(2,1)S(1)} %shard_map.49.own_ref), channel_id=1, source_target_pairs={{0,8},{8,16},{16,24},{24,32},{32,40},{40,48},{48,56},{56,64},{64,7... | collective-permute-start | bytes 589832 | tf_op jit(solution)/shard_map/ppermute | solution.py:232
  58.1 2.7 %shard_map.50.toe_ref = bf16[16,2432,128]{2,1,0:T(8,128)(2,1)S(1)} custom-call(bf16[768,128]{1,0:T(8,128)(2,1)S(1)} %shard_map.49.own_ref), custom_call_target="tpu_custom_call" | custom-call | flops 2550136832 | bytes 10158080 | tf_op jit(solution)/shard_map/pallas_call | solution.py:207
  60.8 0.0 collective-permute-done.1.right_ref
  60.8 5.8 %collective-permute-done.left_ref = bf16[768,128]{1,0:T(8,128)(2,1)S(1)} collective-permute-done((bf16[768,128]{1,0:T(8,128)(2,1)S(1)}, bf16[768,128]{1,0:T(8,128)(2,1)S(1)}, u32[]{:S(2)}, u32[]{:S(2)}) %collective-permute-start) | collective-permute-done | bytes 196640 | tf_op jit(solution)/shard_map/ppermute | solution.py:232
  66.6 5.7 %shard_map.51 = f32[9,16,2001]{2,1,0:T(8,128)} custom-call(s32[32]{0:T(128)S(1)} %pad_add_fusion.place_ref, bf16[16,2432,128]{2,1,0:T(8,128)(2,1)S(1)} %shard_map.50.toe_ref, bf16[768,128]{1,0:T(8,128)(2,1)S(1)} %collective-permute-done.left_ref, bf16[768,128]{1,0:T(8,128)(2,1)S(1)} %shard_map.49.own_ref, bf16[768,128]{1,0:T(8,128)(2,1)S(1)} %collective-permute-done.1.right_ref), custom_call_target="tpu_custom_call" | custom-call | flops 1509949440 | bytes 11704000 | tf_op jit(solution)/shard_map/pallas_call | solution.py:207
  (5 shorter events, 0.1 us)
Async XLA Ops:
  0.0 0.8 %copy-start = (bf16[4,8192]{1,0:T(4,128)(2,1)S(1)}, bf16[4,8192]{1,0:T(4,128)(2,1)}, u32[]{:S(2)}) copy-start(bf16[4,8192]{1,0:T(4,128)(2,1)} %x_ref.1) | copy-start | bytes 196612
  1.6 35.9 %all-to-all-start = ((bf16[64,3,4,128]{3,2,1,0:T(4,128)(2,1)}), bf16[64,3,4,128]{3,2,1,0:T(4,128)(2,1)S(1)}, u32[]{:S(2)}, u32[]{:S(2)}) async-start(bf16[64,3,4,128]{3,2,1,0:T(4,128)(2,1)} %shard_map.47), calls=%async_computation | async-start | bytes 393216 | tf_op jit(solution)/shard_map/all_to_all | solution.py:221
  38.5 12.7 %all-to-all-start.1 = ((bf16[8,48,256]{2,1,0:T(8,128)(2,1)}), bf16[8,48,256]{2,1,0:T(8,128)(2,1)S(1)}, u32[]{:S(2)}, u32[]{:S(2)}) async-start(bf16[8,48,256]{2,1,0:T(8,128)(2,1)} %shard_map.48), calls=%async_computation.1 | async-start | bytes 393216 | tf_op jit(solution)/shard_map/all_to_all | solution.py:226
  52.3 8.5 %collective-permute-start.1 = (bf16[768,128]{1,0:T(8,128)(2,1)S(1)}, bf16[768,128]{1,0:T(8,128)(2,1)S(1)}, u32[]{:S(2)}, u32[]{:S(2)}) collective-permute-start(bf16[768,128]{1,0:T(8,128)(2,1)S(1)} %shard_map.49.own_ref), channel_id=1, source_target_pairs={{0,504},{8,0},{16,8},{24,16},{32,24},{40,32},{48,40},{56,48},{64,5... | collective-permute-start | bytes 589832 | tf_op jit(solution)/shard_map/ppermute | solution.py:231
  56.2 10.4 %collective-permute-start = (bf16[768,128]{1,0:T(8,128)(2,1)S(1)}, bf16[768,128]{1,0:T(8,128)(2,1)S(1)}, u32[]{:S(2)}, u32[]{:S(2)}) collective-permute-start(bf16[768,128]{1,0:T(8,128)(2,1)S(1)} %shard_map.49.own_ref), channel_id=1, source_target_pairs={{0,8},{8,16},{16,24},{24,32},{32,40},{40,48},{48,56},{56,64},{64,7... | collective-permute-start | bytes 589832 | tf_op jit(solution)/shard_map/ppermute | solution.py:232
